TPU v7x, 512 devices: a whole 4x8x8 slice. The times are simulated.
512 devices in a mesh: pair: 16 (over y, core), ri: 8 (over z), batch: 4 (over x).
Axes of the slice: x: 4, y: 8, z: 8, core: 2. Of those that a mesh axis runs over, the one named last changes fastest.
Arguments:
- three_centre: float32 [512, 16, 128, 128], P('pair', 'ri'), may hold values from -0.13258252 to 0.13258252
- pair_mu: int32 [512], P('pair'), may hold values from 0 to 15
- pair_nu: int32 [512], P('pair'), may hold values from 0 to 15
- live_counts: int32 [16], P('pair'), may hold values from 1 to 32, 320 in all
- orbitals: float32 [2048, 512], P('pair', 'batch'), may hold values from -0.5 to 0.5
- metric: float32 [16, 16], P('ri'), may hold values from -1.5 to 1.5
Outputs:
- exchange_blocks: float32 [512, 128, 128], P('pair', ('ri', 'batch'))
Inputs may be any that keep to these rules, and one draw needn't show every extreme that they name: `live_counts`: live slots of each list; the busiest list is full.
All inputs are finite; a program needn't handle non-finite values. No bound on the sum of `live_counts` on one device may be relied on, other than what follows from the above.
Results may differ from a plain program's by a relative error of at most 0.0001.
Values sent between devices are 32-bit elements; how exact they have to be, the bound alone decides.
A program may use at most 64 MiB of HBM per device.

v0:
```python
import jax
import jax.numpy as jnp
from jax import lax
from jax.sharding import PartitionSpec as P

highest = lax.Precision.HIGHEST
per_turn = 8


def per_device(three_centre, pair_mu, pair_nu, live_counts, orbitals, metric):
    list_length = three_centre.shape[0]
    ri_local = three_centre.shape[1]
    block_size = three_centre.shape[2]
    occupied = orbitals.shape[1]
    all_orbitals = lax.all_gather(orbitals, "pair", axis=0, tiled=True)
    block_count = all_orbitals.shape[0] // block_size
    orbital_blocks = all_orbitals.reshape(block_count, block_size, occupied)
    live_count = live_counts[0]
    alive_mask = (jnp.arange(list_length, dtype=jnp.int32) < live_count).astype(jnp.float32)
    mu_selector = (pair_mu[:, None] == jnp.arange(block_count, dtype=jnp.int32)[None, :]).astype(
        jnp.float32
    ) * alive_mask[:, None]
    turn_count = (live_count + per_turn - 1) // per_turn

    def add_group(turn_index, partials):
        first_entry = turn_index * per_turn
        tensor_part = lax.dynamic_slice_in_dim(three_centre, first_entry, per_turn, 0)
        nu_index = lax.dynamic_slice_in_dim(pair_nu, first_entry, per_turn, 0)
        nu_rows = orbital_blocks[nu_index]
        selector = lax.dynamic_slice_in_dim(mu_selector, first_entry, per_turn, 0)
        product = jnp.einsum("kpmn,kni->kpmi", tensor_part, nu_rows, precision=highest)
        return partials + jnp.einsum("ka,kpmi->apmi", selector, product, precision=highest)

    start_sums = jnp.zeros((block_count, ri_local, block_size, occupied), jnp.float32)
    partials = lax.fori_loop(0, turn_count, add_group, start_sums)
    half_transformed = lax.psum_scatter(partials, "pair", scatter_dimension=0, tiled=True)
    fitted = jnp.einsum(
        "qp,apmi->aqmi",
        metric,
        lax.all_gather(half_transformed, "ri", axis=1, tiled=True),
        precision=highest,
    )
    all_fitted = lax.all_gather(fitted, "pair", axis=0, tiled=True)

    def one_turn(turn_index, local_blocks):
        first_entry = turn_index * per_turn
        left_side = all_fitted[lax.dynamic_slice_in_dim(pair_mu, first_entry, per_turn, 0)]
        right_side = all_fitted[lax.dynamic_slice_in_dim(pair_nu, first_entry, per_turn, 0)]
        kept_mask = lax.dynamic_slice_in_dim(alive_mask, first_entry, per_turn, 0)
        product = (
            jnp.einsum("kqmi,kqni->kmn", left_side, right_side, precision=highest)
            * kept_mask[:, None, None]
        )
        return lax.dynamic_update_slice_in_dim(local_blocks, product, first_entry, 0)

    local_blocks = lax.fori_loop(
        0, turn_count, one_turn, jnp.zeros((list_length, block_size, block_size), jnp.float32)
    )
    return lax.psum_scatter(local_blocks, ("ri", "batch"), scatter_dimension=1, tiled=True)


def solution(mesh):
    in_specs = (
        P("pair", "ri", None, None),
        P("pair"),
        P("pair"),
        P("pair"),
        P("pair", "batch"),
        P("ri", None),
    )
    out_specs = P("pair", ("ri", "batch"), None)
    return jax.shard_map(
        per_device, mesh=mesh, in_specs=in_specs, out_specs=out_specs, check_vma=False
    )
```

profile of v0, /device:TPU:1, one launch (start us, length us, event | category | flops | bytes accessed | tf_op | source)
XLA Modules:
  0.0 487.0 jit_solution(15116534012309837884)
XLA Ops:
  6.5 0.7 all-gather.4.cloned.1.call-update
  8.0 0.7 fusion.11
  8.7 47.5 %all-gather.4.cloned.1.call-done = f32[2048,128]{1,0:T(8,128)} async-done(((f32[128,128]{1,0:T(8,128)}), f32[2048,128]{1,0:T(8,128)}) %all-gather.4.cloned.1.call-update) | async-done | bytes 1048592 | tf_op jit(solution)/shard_map/all_gather | solution.py:15
  56.2 0.1 broadcast_in_dim.20
  56.4 14.2 %while.20 = (s32[]{:T(128)}, f32[16,2,128,128]{3,0,2,1:T(8,128)S(1)}, s32[]{:T(128)}, f32[32,16]{1,0:T(8,128)S(1)}, f32[32,2,128,128]{3,2,1,0:T(8,128)}, /*index...) while((s32[]{:T(128)}, ...), condition=%wide.region_1.2_spmd, body=%wide.region_0.1_spmd.sunk | while | flops 453510176 | bytes 8921383 | solution.py:35
  56.4 0.1 compare_select_fusion.5
  56.5 1.8 gather_fusion
  58.3 2.3 fusion.27
  60.6 2.8 convolution_add_fusion.2
  63.5 0.1 compare_select_fusion.5
  63.6 1.8 gather_fusion
  65.4 2.3 fusion.27
  67.7 2.8 convolution_add_fusion.2
  70.6 2.0 copy.9
  72.6 72.7 %reduce-scatter.3.cloned.1.call-done = f32[1,2,128,128]{3,2,1,0:T(8,128)} async-done(((f32[16,2,128,128]{3,2,1,0:T(8,128)}), f32[1,2,128,128]{3,2,1,0:T(8,128)}) %reduce-scatter.3.cloned.1.call-update) | async-done | bytes 131088 | tf_op jit(solution)/shard_map/reduce_scatter | solution.py:36
  145.4 40.5 %all-gather.6.cloned.1.call-done = f32[1,16,128,128]{3,2,0,1:T(8,128)} async-done(((f32[1,2,128,128]{3,2,0,1:T(8,128)}), f32[1,16,128,128]{3,2,0,1:T(8,128)}) %all-gather.6.cloned.1.call-update) | async-done | bytes 1048592 | tf_op jit(solution)/shard_map/all_gather | solution.py:40
  185.9 2.4 convolution_bitcast_fusion.1
  188.3 0.7 copy.12
  189.0 45.1 %all-gather.8.cloned.1.call-done = f32[16,2,128,128]{3,2,1,0:T(8,128)} async-done(((f32[1,2,128,128]{3,2,1,0:T(8,128)}), f32[16,2,128,128]{3,2,1,0:T(8,128)}) %all-gather.8.cloned.1.call-update) | async-done | bytes 2097168 | tf_op jit(solution)/shard_map/all_gather | solution.py:43
  234.1 1.6 broadcast_in_dim.19.clone
  235.7 13.8 %while.21 = (s32[]{:T(128)}, f32[32,128,128]{2,0,1:T(8,128)}, s32[]{:T(128)}, s32[32]{0:T(128)S(1)}, f32[16,2,128,128]{3,2,1,0:T(8,128)}, /*index=5*/s32[32]{0:T...) while((s32[]{:T(128)}, f32[32,128,128]{2,0,1:T(8,128)}, s32[]{:T(128)}, ...), condition=%wide.region_4.5_spmd, body=%wide.region_3.4_spmd.sunk | while | flops 402786368 | bytes 7873031 | solution.py:56
  235.8 0.1 compare_select_fusion.6
  235.9 2.2 gather_fusion.2
  238.1 2.2 gather_fusion.1
  240.3 1.1 fusion.30
  241.4 1.1 copy_dynamic-update-slice_fusion.2
  242.7 2.2 gather_fusion.2
  245.0 2.2 gather_fusion.1
  247.2 1.1 fusion.30
  248.3 1.2 copy_dynamic-update-slice_fusion.2
  249.5 229.4 %reduce-scatter.5.cloned.1.call-done = f32[32,4,128]{2,0,1:T(8,128)} async-done(((f32[32,128,128]{2,0,1:T(8,128)}), f32[32,4,128]{2,0,1:T(8,128)}) %reduce-scatter.5.cloned.1.call-update) | async-done | bytes 65552 | tf_op jit(solution)/shard_map/reduce_scatter | solution.py:59
  478.9 1.5 copy.14
  (25 shorter events, 0.5 us)
Async XLA Ops:
  6.5 179.3 %copy-start = (f32[2,16]{1,0:T(2,128)S(1)}, f32[2,16]{1,0:T(2,128)}, u32[]{:S(2)}) copy-start(f32[2,16]{1,0:T(2,128)} %param.15) | copy-start | bytes 388
  6.5 49.8 %copy-start.2 = (s32[32]{0:T(128)S(1)}, s32[32]{0:T(128)}, u32[]{:S(2)}) copy-start(s32[32]{0:T(128)} %param.12) | copy-start | bytes 388
  6.5 49.7 %all-gather.4.cloned.1.call-start = ((), (), s32[]{:S(2)}) async-start(), calls=%async_computation.2 | async-start | bytes 1114112 | tf_op jit(solution)/shard_map/all_gather | solution.py:15
  7.3 138.1 %reduce-scatter.3.cloned.1.call-start = ((), (), s32[]{:S(2)}) async-start(), calls=%async_computation.3 | async-start | bytes 2228224 | tf_op jit(solution)/shard_map/reduce_scatter | solution.py:36
  72.6 163.1 %copy-start.1 = (s32[32]{0:T(128)S(1)}, s32[32]{0:T(128)}, u32[]{:S(2)}) copy-start(s32[32]{0:T(128)} %param.11) | copy-start | bytes 388
  72.6 113.3 %all-gather.6.cloned.1.call-start = ((), (), s32[]{:S(2)}) async-start(), calls=%async_computation.4 | async-start | bytes 1179648 | tf_op jit(solution)/shard_map/all_gather | solution.py:40
  145.3 88.8 %all-gather.8.cloned.1.call-start = ((), (), s32[]{:S(2)}) async-start(), calls=%async_computation.5 | async-start | bytes 2228224 | tf_op jit(solution)/shard_map/all_gather | solution.py:43
  189.0 289.9 %reduce-scatter.5.cloned.1.call-start = ((), (), s32[]{:S(2)}) async-start(), calls=%async_computation.6 | async-start | bytes 2162688 | tf_op jit(solution)/shard_map/reduce_scatter | solution.py:59
Sparse Core Ops, SparseCore 0:
  9.5 46.6 all-gather.3
  72.7 72.5 reduce-scatter.2
  147.4 38.4 all-gather.5
  189.1 44.9 all-gather.7
  249.6 229.2 reduce-scatter.4
where the time goes:
time: 492 us; the launch traced here: 487 us
  waiting for transfers between devices  436 us (89%)
  local copies, waits for them, and re-layouts  20.7 us (4%)
  matrix products  15 us (3%)
  between operations  13.9 us (3%)
    reduce_scatter x1, waiting for transfers between devices, per_device(): lax.psum_scatter(local_blocks, ('ri', 'batch'), scatter_dimension=1, tile...  229 us
    reduce_scatter x1, waiting for transfers between devices, per_device(): lax.psum_scatter(partials, 'pair', scatter_dimension=0, tiled=True)  72.7 us
    all_gather x1, waiting for transfers between devices, per_device(): all_orbitals = lax.all_gather(orbitals, 'pair', axis=0, tiled=True)  47.5 us
    all_gather x1, waiting for transfers between devices, per_device(): all_fitted = lax.all_gather(fitted, 'pair', axis=0, tiled=True)  45.1 us
    all_gather x1, waiting for transfers between devices, per_device(): lax.all_gather(half_transformed, 'ri', axis=1, tiled=True)  40.5 us
  transfers between devices with their start and end apart: 5, of which 5 were waited for; matrix products, arithmetic and copies ran while one was open for 0% of the time, Pallas kernels for 0%

commit v1 on v0

v1 whole, which is shorter than its diff:
```python
import functools

import jax
import jax.numpy as jnp
from jax import lax
from jax.experimental import pallas as pl
from jax.experimental.pallas import tpu as pltpu
from jax.sharding import PartitionSpec as P

MESH = pl.DeviceIdType.MESH
F32 = jnp.float32
BF16 = jnp.bfloat16
SLOTS = 32
NB = 16
BS = 128
NY, NZ, NX = 8, 8, 4
GROUP = 4
NEAR_FIRST = (1, 7, 2, 6, 3, 5, 4)
FAR_FIRST = (4, 3, 5, 2, 6, 1, 7, 0)


def split(x):
    hi = x.astype(BF16)
    return hi, (x - hi.astype(F32)).astype(BF16)


def mm(a, b, nt):
    dims = (((1,), (1 if nt else 0,)), ((), ()))
    return lax.dot_general(a, b, dims, preferred_element_type=F32)


def dot3(a, b, nt=False):
    (ah, al), (bh, bl) = a, b
    return mm(ah, bh, nt) + (mm(ah, bl, nt) + mm(al, bh, nt))


def kernel(
    mu_s, nu_s, prev_s, last_s, live_s, t_any, c_ref, kr_ref, o_ref,
    t_v, t_hi, t_lo, run, c_raw, c_hi, c_lo, kr_all, d_send, d_recv, ring, ho, hz, lb, rb, pk, xr, kf,
    t_sem, a_s, a_r, ad_s, ad_r, m_s, m_r, d_s, d_r, g_s, g_r, z_s, z_r,
    fy_s, fy_r, fz_s, fz_r, fd_s, fd_r, x_s, x_r, k_s, k_r, kd_s, kd_r,
):
    p, q, b = lax.axis_index("pair"), lax.axis_index("ri"), lax.axis_index("batch")
    y, c = p // 2, lax.rem(p, 2)

    def ypos(d):
        return lax.rem(y + d + NY, NY)

    def ydev(d):
        return (ypos(d) * 2 + c, q, b)

    def zpos(d):
        return lax.rem(q + d + NZ, NZ)

    def zdev(d):
        return (p, zpos(d), b)

    def xdev(d):
        return (p, q, lax.rem(b + d + NX, NX))

    partner = (y * 2 + 1 - c, q, b)
    sent = []

    def send(src, dst, ss, rs, dev):
        cp = pltpu.make_async_remote_copy(
            src_ref=src, dst_ref=dst, send_sem=ss, recv_sem=rs, device_id=dev, device_id_type=MESH
        )
        cp.start()
        sent.append(cp)
        return cp

    t_copy = pltpu.make_async_copy(t_any, t_v, t_sem)
    t_copy.start()
    barrier = pltpu.get_barrier_semaphore()
    peers = [ydev(d) for d in range(1, NY)] + [zdev(d) for d in range(1, NZ)]
    peers += [xdev(d) for d in range(1, NX)] + [partner]
    for dev in peers:
        pl.semaphore_signal(barrier, inc=1, device_id=dev, device_id_type=MESH)
    pl.semaphore_wait(barrier, len(peers))

    a_cp = {d: send(c_ref, c_raw.at[p], a_s.at[d], a_r.at[d], ydev(d)) for d in NEAR_FIRST}
    ad_cp = {0: send(c_ref, c_raw.at[p], ad_s.at[0], ad_r.at[0], partner)}
    m_cp = {d: send(kr_ref, kr_all.at[q], m_s.at[d], m_r.at[d], zdev(d)) for d in NEAR_FIRST}
    kr_all[q] = kr_ref[...]
    c_hi[p], c_lo[p] = split(c_ref[...])
    t_copy.wait()

    def split_t(k, carry):
        t_hi[k], t_lo[k] = split(t_v[k].reshape(2 * BS, BS))
        return carry

    lax.fori_loop(0, SLOTS, split_t, 0)
    run[SLOTS] = jnp.zeros((2 * BS, BS), F32)

    def take_c(i):
        c_hi[i], c_lo[i] = split(c_raw[i])

    for d in NEAR_FIRST:
        i = ypos(-d) * 2 + c
        a_cp[d].wait_recv()
        ad_cp[d] = send(c_raw.at[i], c_raw.at[i], ad_s.at[d], ad_r.at[d], partner)
        take_c(i)
    for d in (0,) + NEAR_FIRST:
        ad_cp[d].wait_recv()
        take_c(ypos(-d) * 2 + 1 - c)

    def add_slots(g, carry):
        products = []
        for j in range(GROUP):
            k = g * GROUP + j
            nu = nu_s[k]
            products.append(dot3((t_hi[k], t_lo[k]), (c_hi[nu], c_lo[nu])))
        for j in range(GROUP):
            k = g * GROUP + j
            run[k] = products[j] + run[prev_s[k]]
        return carry

    lax.fori_loop(0, SLOTS // GROUP, add_slots, 0)

    d_cp = {}
    for off in FAR_FIRST:
        d_send[off] = run[last_s[ypos(off) * 2 + 1 - c]].reshape(2, BS, BS)
        d_cp[off] = send(d_send.at[off], d_recv.at[off], d_s.at[off], d_r.at[off], partner)

    def add_core(off):
        d_cp[off].wait_recv()
        d_recv[off] = d_recv[off] + run[last_s[ypos(off) * 2 + c]].reshape(2, BS, BS)

    half = BS // 2
    g_cp = {}
    add_core(4)
    for s in range(1, 5):
        for way in (0, 1):
            off = 5 - s if way == 0 else 3 + s
            if s > 1:
                add_core(off)
            for part in (0, 1):
                if s > 1:
                    g_cp[part, way, s - 1].wait_recv()
                rows = pl.ds(half * way, half) if s <= 2 else pl.ds(0, BS)
                if s > 1:
                    d_recv[off, part, rows, :] = d_recv[off, part, rows, :] + ring[part, way, s - 2, rows, :]
                if s > 1:
                    rows = pl.ds(0, BS)
                n = (part * 2 + way) * 4 + s - 1
                g_cp[part, way, s] = send(
                    d_recv.at[off, part, rows], ring.at[part, way, s - 1, rows],
                    g_s.at[n], g_r.at[n], ydev(1 if way == 0 else -1),
                )
    add_core(0)
    for part in (0, 1):
        for way in (0, 1):
            g_cp[part, way, 4].wait_recv()
        ho[part] = d_recv[0, part] + (ring[part, 0, 3] + ring[part, 1, 3])

    z_cp = {}
    for d in NEAR_FIRST:
        rows = pl.ds(pl.multiple_of(zpos(d) * 16, 16), 16)
        z_cp[d] = send(ho.at[:, rows], hz.at[q], z_s.at[d], z_r.at[d], zdev(d))
    hz[q] = ho[:, pl.ds(pl.multiple_of(q * 16, 16), 16), :]
    for d in NEAR_FIRST:
        m_cp[d].wait_recv()
    mixer = split(kr_all[...].reshape(256, 256))
    for d in NEAR_FIRST:
        z_cp[d].wait_recv()
    fitted = dot3(mixer, split(hz[...].reshape(256, BS)))
    lb[p] = fitted
    rb[q] = fitted

    f_cp = {}
    fd_cp = {}

    def hops(way, part):
        return 4 if way == part else 3

    def fitted_slot(axis, way, s):
        d = 1 - s if way == 0 else s - 1
        return ypos(d) * 2 + c if axis == 0 else zpos(d)

    def to_partner(way, part, s):
        rows = pl.ds(part * BS, BS)
        i = fitted_slot(0, way, s)
        n = (4 + (1 - s if way == 0 else s - 1)) % 8 * 2 + part
        fd_cp[n] = send(lb.at[i, rows], lb.at[i, rows], fd_s.at[n], fd_r.at[n], partner)

    for s in range(1, 6):
        for part in (0, 1):
            for way in (part, 1 - part):
                if s > hops(way, part) + 1:
                    continue
                for axis in (0, 1):
                    if s > 1:
                        f_cp[axis, way, part, s - 1].wait_recv()
                    if s <= hops(way, part):
                        rows = pl.ds(part * BS, BS)
                        i = fitted_slot(axis, way, s)
                        buf, ss, rs = ((lb, fy_s, fy_r), (rb, fz_s, fz_r))[axis]
                        n = (part * 2 + way) * 4 + s - 1
                        step = 1 if way == 0 else -1
                        f_cp[axis, way, part, s] = send(
                            buf.at[i, rows], buf.at[i, rows], ss.at[n], rs.at[n],
                            ydev(step) if axis == 0 else zdev(step),
                        )
                if s > 1 or way == 0:
                    to_partner(way, part, s)
    for n in sorted(fd_cp):
        fd_cp[n].wait_recv()

    def add_q(i, acc):
        rows = pl.ds(pl.multiple_of(i * 16, 16), 16)
        left = lb[:, rows, :].reshape(256, BS)
        right = rb[:, rows, :].reshape(BS, BS)
        return acc + dot3(split(left), split(right), nt=True)

    k_part = lax.fori_loop(0, 16, add_q, jnp.zeros((256, BS), F32))
    tiles = k_part.reshape(16, 2, 8, BS)
    low = lax.broadcasted_iota(jnp.int32, (8, BS), 0) < 4
    for j in range(NX):
        for pair in range(8):
            first, second = tiles[2 * pair, j // 2], tiles[2 * pair + 1, j // 2]
            if j % 2 == 0:
                tile = jnp.where(low, first, pltpu.roll(second, 4, 0))
            else:
                tile = jnp.where(low, pltpu.roll(first, 4, 0), second)
            pk[j, pair] = tile
    x_cp = {}
    for d in range(1, NX):
        to = lax.rem(b + d, NX)
        x_cp[d] = send(pk.at[to], xr.at[d], x_s.at[d], x_r.at[d], xdev(d))
    for d in range(1, NX):
        x_cp[d].wait_recv()
    kf[p] = (pk[b] + xr[1]) + (xr[2] + xr[3])

    k_cp = {d: send(kf.at[p], kf.at[p], k_s.at[d], k_r.at[d], ydev(d)) for d in NEAR_FIRST}
    kd_cp = {0: send(kf.at[p], kf.at[p], kd_s.at[0], kd_r.at[0], partner)}
    for d in NEAR_FIRST:
        i = ypos(-d) * 2 + c
        k_cp[d].wait_recv()
        kd_cp[d] = send(kf.at[i], kf.at[i], kd_s.at[d], kd_r.at[d], partner)
    for d in (0,) + NEAR_FIRST:
        kd_cp[d].wait_recv()

    live = live_s[0]
    for k in range(SLOTS):
        mu = mu_s[k]
        tile = kf[nu_s[k], mu >> 1]
        rows = jnp.where(mu & 1 == 1, tile[4:8], tile[0:4])
        o_ref[k] = jnp.where(k < live, rows, jnp.zeros_like(rows))

    for cp in sent:
        cp.wait_send()


def per_device(three_centre, pair_mu, pair_nu, live_counts, orbitals, metric):
    slot = jnp.arange(SLOTS, dtype=jnp.int32)
    alive = slot < live_counts[0]
    same = (pair_mu[:, None] == pair_mu[None, :]) & alive[None, :] & (slot[None, :] < slot[:, None])
    prev = jnp.max(jnp.where(same, slot[None, :], -1), axis=1)
    prev = jnp.where(prev < 0, SLOTS, prev)
    block = jnp.arange(NB, dtype=jnp.int32)
    mine = (pair_mu[None, :] == block[:, None]) & alive[None, :]
    last = jnp.max(jnp.where(mine, slot[None, :], -1), axis=1)
    last = jnp.where(last < 0, SLOTS, last)
    wide = jnp.broadcast_to(metric[:, :, None], (2, 16, 16)).reshape(2, 1, 256)
    row = jnp.arange(16, dtype=jnp.int32)[None, :, None]
    col = jnp.arange(256, dtype=jnp.int32)[None, None, :] % 16
    mixer = jnp.where(row == col, wide, 0.0).reshape(32, 256)
    smem = pl.BlockSpec(memory_space=pltpu.SMEM)
    vmem = pl.BlockSpec(memory_space=pltpu.VMEM)

    def sems(*counts):
        return [pltpu.SemaphoreType.DMA((n,)) for n in counts for _ in range(2)]

    return pl.pallas_call(
        kernel,
        out_shape=jax.ShapeDtypeStruct((SLOTS, 4, BS), F32),
        in_specs=[smem] * 5 + [pl.BlockSpec(memory_space=pl.ANY), vmem, vmem],
        out_specs=vmem,
        scratch_shapes=[
            pltpu.VMEM((SLOTS, 2, BS, BS), F32),
            pltpu.VMEM((SLOTS, 2 * BS, BS), BF16),
            pltpu.VMEM((SLOTS, 2 * BS, BS), BF16),
            pltpu.VMEM((SLOTS + 1, 2 * BS, BS), F32),
            pltpu.VMEM((NB, BS, BS), F32),
            pltpu.VMEM((NB, BS, BS), BF16),
            pltpu.VMEM((NB, BS, BS), BF16),
            pltpu.VMEM((NZ, 32, 256), F32),
            pltpu.VMEM((NY, 2, BS, BS), F32),
            pltpu.VMEM((NY, 2, BS, BS), F32),
            pltpu.VMEM((2, 2, 4, BS, BS), F32),
            pltpu.VMEM((2, BS, BS), F32),
            pltpu.VMEM((NZ, 2, 16, BS), F32),
            pltpu.VMEM((NB, 256, BS), F32),
            pltpu.VMEM((NZ, 256, BS), F32),
            pltpu.VMEM((NX, 8, 8, BS), F32),
            pltpu.VMEM((NX, 8, 8, BS), F32),
            pltpu.VMEM((NB, 8, 8, BS), F32),
            pltpu.SemaphoreType.DMA,
        ]
        + sems(8, 8, 8, 8, 16, 8, 16, 16, 16, 4, 8, 8),
        compiler_params=pltpu.CompilerParams(
            collective_id=0, has_side_effects=True, vmem_limit_bytes=48 * 2**20
        ),
        name="exchange",
    )(pair_mu, pair_nu, prev, last, live_counts, three_centre, orbitals, mixer)


def solution(mesh):
    in_specs = (
        P("pair", "ri", None, None),
        P("pair"),
        P("pair"),
        P("pair"),
        P("pair", "batch"),
        P("ri", None),
    )
    return jax.shard_map(
        per_device,
        mesh=mesh,
        in_specs=in_specs,
        out_specs=P("pair", ("ri", "batch"), None),
        check_vma=False,
    )
```

time: 492 us -> 103 us (0.21); the launches traced: 487 us -> 103 us
  waiting for transfers between devices: 436 us -> 0 us
  Pallas kernels: 0 us -> 94.7 us
  matrix products: 15 us -> 0 us
  local copies, waits for them, and re-layouts: 20.7 us -> 5.8 us
  between operations: 13.9 us -> 0.71 us
    reduce_scatter x2 -> x0, waiting for transfers between devices: 302 us -> none  [the longest x1 229 us: per_device(): lax.psum_scatter(local_blocks, ('ri', 'batch'), scatter_dimension=1, tile...]
    all_gather x3 -> x0, waiting for transfers between devices: 133 us -> none  [the longest x1 47.5 us: per_device(): all_orbitals = lax.all_gather(orbitals, 'pair', axis=0, tiled=True)]
    pallas_call x0 -> x1, Pallas kernels: none -> 94.7 us  [per_device(): pl.pallas_call(kernel, out_shape=jax.ShapeDtypeStruct((SLOTS, 4, BS), F32...]
    dot_general x7 -> x0, matrix products: 15 us -> none  [the longest x2 5.68 us: add_group(): jnp.einsum('ka,kpmi->apmi', selector, product, precision=highest)]
    gather x6 -> x0, local copies, waits for them, and re-layouts: 12.4 us -> none  [the longest x2 4.41 us: one_turn(): all_fitted[lax.dynamic_slice_in_dim(pair_mu, first_entry, per_turn, 0)]]
    unnamed x6 -> x9, local copies, waits for them, and re-layouts: 0.01 us -> 4.96 us
  transfers between devices with their start and end apart: 5 -> 0, of which waited for: 5 -> 0; matrix products, arithmetic and copies ran while one was open for 0% -> 0% of each run, Pallas kernels for 0% -> 0%
where the time goes in v1:
time: 103 us
  Pallas kernels  94.7 us (92%)
  local copies, waits for them, and re-layouts  5.8 us (6%)
  other arithmetic  1.73 us (2%)
    pallas_call x1, Pallas kernels, per_device(): pl.pallas_call(kernel, out_shape=jax.ShapeDtypeStruct((SLOTS, 4, BS), F32...  94.7 us
    unnamed x9, local copies, waits for them, and re-layouts  4.96 us

profile of v1, /device:TPU:1, one launch (start us, length us, event | category | flops | bytes accessed | tf_op | source)
XLA Modules:
  0.0 102.9 jit_solution(4927732703095098195)
XLA Ops:
  0.7 0.8 select_reduce_fusion.1
  1.4 0.9 select_reduce_fusion
  2.4 0.8 broadcast_in_dim.76
  3.2 0.1 broadcast_in_dim.77
  3.3 0.0 copy-start
  3.3 2.2 %copy-done = f32[32,2,128,128]{3,2,1,0:T(8,128)S(1)} copy-done((f32[32,2,128,128]{3,2,1,0:T(8,128)S(1)}, f32[32,2,128,128]{3,2,1,0:T(8,128)}, u32[]{:S(2)}) %copy-start) | copy-done | bytes 4194328
  5.4 0.0 copy-start.1
  5.4 0.8 copy-done.1
  6.3 0.0 copy-start.2
  6.3 0.7 copy-done.2
  6.9 0.0 copy-start.3
  6.9 0.7 copy-done.3
  7.6 94.7 %exchange.1 = f32[32,4,128]{2,1,0:T(4,128)S(1)} custom-call(s32[32]{0:T(128)S(1)} %copy-done.2, s32[32]{0:T(128)S(1)} %copy-done.3, s32[32]{0:T(128)S(1)} %compare_select_fusion.1.prev_s, s32[16]{0:T(128)S(1)} %compare_select_fusion.last_s, s32[1]{0:T(128)} %copy.8.live_s, f32[32,2,128,128]{3,2,1,0:T(8,128)S(1)} %copy-done, f32[128,128]{1,0:T(8,128)S(1)} %copy-done.1, ...), custom_call_target="tpu_custom_call" | custom-call | tf_op jit(solution)/shard_map/exchange/pallas_call | solution.py:274
  102.3 0.6 copy.9
  (6 shorter events, 0.0 us)
Async XLA Ops:
  3.3 2.2 %copy-start = (f32[32,2,128,128]{3,2,1,0:T(8,128)S(1)}, f32[32,2,128,128]{3,2,1,0:T(8,128)}, u32[]{:S(2)}) copy-start(f32[32,2,128,128]{3,2,1,0:T(8,128)} %t_any.1) | copy-start | bytes 12582916
  5.4 0.8 copy-start.1
  6.3 0.7 copy-start.2
  6.9 0.7 copy-start.3

commit v2 on v1

v2 whole, which is shorter than its diff:
```python
import jax
import jax.numpy as jnp
from jax import lax
from jax.experimental import pallas as pl
from jax.experimental.pallas import tpu as pltpu
from jax.sharding import PartitionSpec as P

MESH = pl.DeviceIdType.MESH
F32 = jnp.float32
BF16 = jnp.bfloat16
SLOTS = 32
NB = 16
BS = 128
NY, NZ, NX = 8, 8, 4
GROUP = 4
NEAR_FIRST = (1, 7, 2, 6, 3, 5, 4)


def split(x):
    hi = x.astype(BF16)
    return hi, (x - hi.astype(F32)).astype(BF16)


def mm(a, b, nt=False):
    dims = (((1,), (1 if nt else 0,)), ((), ()))
    return lax.dot_general(a, b, dims, preferred_element_type=F32)


def kernel(
    mu_any, nu_any, live_any, t_any, c_any, m_any, o_ref,
    mu_s, nu_s, live_s, prev_s, last_s,
    t_v, t_cat, run, c_raw, c_cat, m_v, kr_own, kr_all, mix, d_send, d_recv, ring, ho, hz, lb, rb, l_cat, r_cat,
    pk, xr, kf,
    in_sem, a_s, a_r, ad_s, ad_r, m_s, m_r, d_s, d_r, g_s, g_r, z_s, z_r,
    fy_s, fy_r, fz_s, fz_r, fd_s, fd_r, x_s, x_r, k_s, k_r, kd_s, kd_r,
):
    p, q, b = lax.axis_index("pair"), lax.axis_index("ri"), lax.axis_index("batch")
    y, c = p // 2, lax.rem(p, 2)

    def ypos(d):
        return lax.rem(y + d + NY, NY)

    def ydev(d):
        return (ypos(d) * 2 + c, q, b)

    def zpos(d):
        return lax.rem(q + d + NZ, NZ)

    def zdev(d):
        return (p, zpos(d), b)

    def xdev(d):
        return (p, q, lax.rem(b + d + NX, NX))

    partner = (y * 2 + 1 - c, q, b)
    sent = []

    def send(src, dst, ss, rs, dev):
        cp = pltpu.make_async_remote_copy(
            src_ref=src, dst_ref=dst, send_sem=ss, recv_sem=rs, device_id=dev, device_id_type=MESH
        )
        cp.start()
        sent.append(cp)
        return cp

    def drain(keep=0):
        while len(sent) > keep:
            sent.pop(0).wait_send()

    def block(d):
        return ypos(d) * 2 + c

    def other(d):
        return ypos(d) * 2 + 1 - c

    class Gather:
        def __init__(self, own, buf, half, sems):
            self.buf, self.half, self.sems = buf, half, sems
            ss, rs, ds, dr = sems
            self.cp = {d: send(own, buf.at[p], ss.at[i], rs.at[i], ydev(d)) for i, d in enumerate((2, -2, 1, -1))}
            self.dp = {0: send(own, buf.at[p], ds.at[0], dr.at[0], partner)}

        def relay(self, d):
            step = d // 2
            ss, rs, _, _ = self.sems
            self.cp[d].wait_recv()
            n = 4 if step == 1 else 5
            at = self.buf.at[block(-d)]
            self.cp[3 * step] = send(at, at, ss.at[n], rs.at[n], ydev(step))
            rows = pl.ds(0 if step == 1 else self.half, self.half)
            part = self.buf.at[block(-d), rows]
            self.cp[4 * step] = send(part, part, ss.at[n + 2], rs.at[n + 2], ydev(d))
            self.share(d)

        def share(self, d):
            _, _, ds, dr = self.sems
            at = self.buf.at[block(-d)]
            self.dp[d] = send(at, at, ds.at[d % 8], dr.at[d % 8], partner)

        def take(self, d):
            self.cp[d].wait_recv()
            if d == 4:
                self.cp[-4].wait_recv()
            self.share(d)

        def shared(self, d):
            self.dp[d].wait_recv()

    ins = [
        pltpu.make_async_copy(src, dst, in_sem.at[i])
        for i, (src, dst) in enumerate(
            ((c_any, c_raw.at[p]), (mu_any, mu_s), (nu_any, nu_s), (live_any, live_s), (m_any, m_v), (t_any, t_v))
        )
    ]
    for cp in ins:
        cp.start()
    barrier = pltpu.get_barrier_semaphore()
    peers = [ydev(d) for d in (1, -1, 2, -2)] + [zdev(d) for d in range(1, NZ)]
    peers += [xdev(d) for d in range(1, NX)] + [partner]
    for dev in peers:
        pl.semaphore_signal(barrier, inc=1, device_id=dev, device_id_type=MESH)
    pl.semaphore_wait(barrier, len(peers))

    orbs = Gather(c_any, c_raw, BS // 2, (a_s, a_r, ad_s, ad_r))
    ins[4].wait()
    col = lax.broadcasted_iota(jnp.int32, (16, 256), 1)
    spot = (col % 16) == lax.broadcasted_iota(jnp.int32, (16, 256), 0)
    for j in range(2):
        wide = jnp.zeros((16, 256), F32)
        for i in range(16):
            wide = jnp.where((col >= 16 * i) & spot, m_v[pl.ds(j, 1), pl.ds(i, 1)], wide)
        kr_own[pl.ds(16 * j, 16), :] = wide
    kr_all[q] = kr_own[...]
    m_cp = {d: send(kr_own, kr_all.at[q], m_s.at[d], m_r.at[d], zdev(d)) for d in NEAR_FIRST}

    for i in (1, 2, 3):
        ins[i].wait()
    live = live_s[0]

    def link_slot(k, carry):
        mine = mu_s[k]
        best = jnp.int32(SLOTS)
        for j in range(SLOTS):
            best = jnp.where((mu_s[j] == mine) & (j < k), jnp.int32(j), best)
        prev_s[k] = best
        return carry

    def link_block(a, carry):
        best = jnp.int32(SLOTS)
        for j in range(SLOTS):
            best = jnp.where((mu_s[j] == a) & (j < live), jnp.int32(j), best)
        last_s[a] = best
        return carry

    lax.fori_loop(0, SLOTS, link_slot, 0)
    lax.fori_loop(0, NB, link_block, 0)

    def take_c(i):
        hi, lo = split(c_raw[i])
        for j in range(2):
            c_cat[i, pl.ds(BS * j, BS), pl.ds(0, BS)] = hi
            c_cat[i, pl.ds(BS * j, BS), pl.ds(BS, BS)] = lo

    def split_t(k, carry):
        hi, lo = split(t_v[k].reshape(2 * BS, BS))
        t_cat[k, :, pl.ds(0, BS)] = hi
        t_cat[k, :, pl.ds(BS, BS)] = lo
        return carry

    ins[5].wait()
    lax.fori_loop(0, 8, split_t, 0)
    for d in (2, -2):
        orbs.relay(d)
    for d in (1, -1):
        orbs.take(d)
    lax.fori_loop(8, SLOTS, split_t, 0)
    ins[0].wait()
    take_c(p)
    for d in (2, -2, 1, -1):
        take_c(block(-d))
    for d in (0, 2, -2, 1, -1):
        orbs.shared(d)
        take_c(other(-d))
    for d in (3, -3, 4):
        orbs.take(d)
        take_c(block(-d))
    run[SLOTS] = jnp.zeros((2 * BS, BS), F32)
    for d in (3, -3, 4):
        orbs.shared(d)
        take_c(other(-d))

    def add_slots(g, carry):
        products = []
        for j in range(GROUP):
            k = g * GROUP + j
            both = mm(t_cat[k], c_cat[nu_s[k]])
            products.append(both[:, :BS] + both[:, BS:])
        for j in range(GROUP):
            k = g * GROUP + j
            run[k] = products[j] + run[prev_s[k]]
        return carry

    lax.fori_loop(0, SLOTS // GROUP, add_slots, 0)

    d_cp = {}
    for off in (4, 3, 5, 2, 6, 1, 7, 0):
        d_send[off] = run[last_s[other(off)]].reshape(2, BS, BS)
        d_cp[off] = send(d_send.at[off], d_recv.at[off], d_s.at[off], d_r.at[off], partner)

    def add_core(off):
        d_cp[off].wait_recv()
        d_recv[off] = d_recv[off] + run[last_s[block(off)]].reshape(2, BS, BS)

    half = BS // 2
    g_cp = {}

    def pass_on(off, part, way, kind, hop):
        rows = pl.ds(half * way, half) if kind == 3 else pl.ds(0, BS)
        n = (part * 2 + way) * 4 + kind
        g_cp[part, way, kind] = send(
            d_recv.at[off, part, rows], ring.at[part, way, kind, rows], g_s.at[n], g_r.at[n],
            ydev(hop if way == 0 else -hop),
        )

    add_core(4)
    for part in (0, 1):
        for way in (0, 1):
            pass_on(4, part, way, 3, 2)
    for way, off in ((0, 3), (1, 5)):
        add_core(off)
        for part in (0, 1):
            pass_on(off, part, way, 0, 1)
    add_core(2)
    add_core(6)
    for part in (0, 1):
        for way, off in ((0, 2), (1, 6)):
            g_cp[part, way, 3].wait_recv()
            rows = pl.ds(half * way, half)
            d_recv[off, part, rows, :] = d_recv[off, part, rows, :] + ring[part, way, 3, rows, :]
            g_cp[part, way, 0].wait_recv()
            d_recv[off, part] = d_recv[off, part] + ring[part, way, 0]
            pass_on(off, part, way, 1, 1)
    add_core(1)
    add_core(7)
    add_core(0)
    for part in (0, 1):
        for way, off in ((0, 1), (1, 7)):
            g_cp[part, way, 1].wait_recv()
            d_recv[off, part] = d_recv[off, part] + ring[part, way, 1]
            pass_on(off, part, way, 2, 1)
    for d in NEAR_FIRST:
        m_cp[d].wait_recv()
    mix_hi, mix_lo = split(kr_all[...].reshape(256, 256))
    mix[0] = mix_hi
    mix[1] = mix_lo

    z_cp = {}
    for part in (0, 1):
        for way in (0, 1):
            g_cp[part, way, 2].wait_recv()
        ho[part] = d_recv[0, part] + (ring[part, 0, 2] + ring[part, 1, 2])
        for d in NEAR_FIRST:
            rows = pl.ds(pl.multiple_of(zpos(d) * 16, 16), 16)
            n = d * 2 + part
            z_cp[n] = send(ho.at[part, rows], hz.at[q, part], z_s.at[n], z_r.at[n], zdev(d))
        hz[q, part] = ho[part, pl.ds(pl.multiple_of(q * 16, 16), 16), :]
    drain(14)
    for n in sorted(z_cp):
        z_cp[n].wait_recv()
    hz_hi, hz_lo = split(hz[...].reshape(256, BS))
    fitted = mm(mix[0], hz_hi) + (mm(mix[0], hz_lo) + mm(mix[1], hz_hi))
    lb[p] = fitted
    rb[q] = fitted

    f_cp = {}
    fd_cp = {}

    def hand_on(axis, way, part, d, kind, hop):
        sign = 1 if way == 0 else -1
        buf, ss, rs = ((lb, fy_s, fy_r), (rb, fz_s, fz_r))[axis]
        i = block(-sign * d) if axis == 0 else zpos(-sign * d)
        at = buf.at[i, pl.ds(part * BS, BS)]
        n = (part * 2 + way) * 4 + kind
        dev = ydev(sign * hop) if axis == 0 else zdev(sign * hop)
        f_cp[axis, way, part, kind] = send(at, at, ss.at[n], rs.at[n], dev)

    def to_partner(d, part):
        at = lb.at[block(-d), pl.ds(part * BS, BS)]
        n = (d % 8) * 2 + part
        fd_cp[d % 8, part] = send(at, at, fd_s.at[n], fd_r.at[n], partner)

    def put_left(i, part):
        hi, lo = split(lb[i, pl.ds(part * BS, BS), :])
        rows = pl.ds(pl.multiple_of(i * 16, 16), 16)
        for j in range(8):
            at = (part * 8 + j) * 256
            l_cat[rows, pl.ds(at, BS)] = hi[16 * j : 16 * j + 16]
            l_cat[rows, pl.ds(at + BS, BS)] = lo[16 * j : 16 * j + 16]

    def put_right(i, part):
        hi, lo = split(rb[i, pl.ds(part * BS, BS), :])
        for s, x in enumerate((hi, lo)):
            rows = pl.ds(pl.multiple_of(i * 16 + BS * s, 16), 16)
            for j in range(8):
                at = (part * 8 + j) * 256
                r_cat[rows, pl.ds(at, BS)] = x[16 * j : 16 * j + 16]
                r_cat[rows, pl.ds(at + BS, BS)] = x[16 * j : 16 * j + 16]

    def put(axis, d, part):
        if axis == 0:
            put_left(block(-d), part)
        else:
            put_right(zpos(-d), part)

    def put_shared(d, part):
        fd_cp[d % 8, part].wait_recv()
        put_left(other(-d), part)

    for part in (0, 1):
        for way in (0, 1):
            for axis in (0, 1):
                hand_on(axis, way, part, 0, 0, 1)
    for part in (0, 1):
        to_partner(0, part)
    for part in (0, 1):
        put(0, 0, part)
        put(1, 0, part)
    for part in (0, 1):
        for way, sign in ((0, 1), (1, -1)):
            for axis in (0, 1):
                f_cp[axis, way, part, 0].wait_recv()
                hand_on(axis, way, part, 1, 1, 1)
                if axis == 0:
                    to_partner(sign, part)
    for part in (0, 1):
        for sign in (1, -1):
            for axis in (0, 1):
                put(axis, sign, part)
        put_shared(0, part)
    for part in (0, 1):
        for way, sign in ((0, 1), (1, -1)):
            for axis in (0, 1):
                f_cp[axis, way, part, 1].wait_recv()
                hand_on(axis, way, part, 2, 2, 1)
                if way == part:
                    hand_on(axis, way, part, 2, 3, 2)
                if axis == 0:
                    to_partner(2 * sign, part)
    for part in (0, 1):
        for sign in (1, -1):
            put_shared(sign, part)
            for axis in (0, 1):
                put(axis, 2 * sign, part)
    for part in (0, 1):
        for kind in (2, 3):
            for way, sign in ((0, 1), (1, -1)):
                if kind == 3 and way != part:
                    continue
                for axis in (0, 1):
                    f_cp[axis, way, part, kind].wait_recv()
                    if axis == 0:
                        to_partner((kind + 1) * sign, part)
                    put(axis, (kind + 1) * sign, part)
        for d in (2, -2):
            put_shared(d, part)

    k_part = None
    for part in (0, 1):
        for d in (3, -3, 4):
            put_shared(d, part)
        lanes = pl.ds(part * 2048, 2048)
        both = mm(l_cat[:, lanes], r_cat[:, lanes], nt=True)
        both = both[:, :BS] + both[:, BS:]
        k_part = both if part == 0 else k_part + both
    tiles = k_part.reshape(16, 2, 8, BS)
    low = lax.broadcasted_iota(jnp.int32, (8, BS), 0) < 4
    for j in range(NX):
        for pair in range(8):
            first, second = tiles[2 * pair, j // 2], tiles[2 * pair + 1, j // 2]
            if j % 2 == 0:
                tile = jnp.where(low, first, pltpu.roll(second, 4, 0))
            else:
                tile = jnp.where(low, pltpu.roll(first, 4, 0), second)
            pk[j, pair] = tile
    x_cp = {}
    for d in range(1, NX):
        to = lax.rem(b + d, NX)
        x_cp[d] = send(pk.at[to], xr.at[d], x_s.at[d], x_r.at[d], xdev(d))
    drain(3)
    for d in range(1, NX):
        x_cp[d].wait_recv()
    kf[p] = (pk[b] + xr[1]) + (xr[2] + xr[3])

    cols = Gather(kf.at[p], kf, 4, (k_s, k_r, kd_s, kd_r))
    for d in (2, -2):
        cols.relay(d)
    for d in (1, -1, 3, -3, 4):
        cols.take(d)
    for d in (0, 2, -2, 1, -1, 3, -3, 4):
        cols.shared(d)

    for k in range(SLOTS):
        mu = mu_s[k]
        tile = kf[nu_s[k], mu >> 1]
        rows = jnp.where(mu & 1 == 1, tile[4:8], tile[0:4])
        o_ref[k] = jnp.where(k < live, rows, jnp.zeros_like(rows))
    drain()


def per_device(three_centre, pair_mu, pair_nu, live_counts, orbitals, metric):
    hbm = pl.BlockSpec(memory_space=pltpu.HBM)

    def sems(*counts):
        return [pltpu.SemaphoreType.DMA((n,)) for n in counts for _ in range(2)]

    return pl.pallas_call(
        kernel,
        out_shape=jax.ShapeDtypeStruct((SLOTS, 4, BS), F32),
        in_specs=[hbm] * 6,
        out_specs=pl.BlockSpec(memory_space=pltpu.VMEM),
        scratch_shapes=[
            pltpu.SMEM((SLOTS,), jnp.int32),
            pltpu.SMEM((SLOTS,), jnp.int32),
            pltpu.SMEM((1,), jnp.int32),
            pltpu.SMEM((SLOTS,), jnp.int32),
            pltpu.SMEM((NB,), jnp.int32),
            pltpu.VMEM((SLOTS, 2, BS, BS), F32),
            pltpu.VMEM((SLOTS, 2 * BS, 2 * BS), BF16),
            pltpu.VMEM((SLOTS + 1, 2 * BS, BS), F32),
            pltpu.VMEM((NB, BS, BS), F32),
            pltpu.VMEM((NB, 2 * BS, 2 * BS), BF16),
            pltpu.VMEM((2, 16), F32),
            pltpu.VMEM((32, 256), F32),
            pltpu.VMEM((NZ, 32, 256), F32),
            pltpu.VMEM((2, 256, 256), BF16),
            pltpu.VMEM((NY, 2, BS, BS), F32),
            pltpu.VMEM((NY, 2, BS, BS), F32),
            pltpu.VMEM((2, 2, 4, BS, BS), F32),
            pltpu.VMEM((2, BS, BS), F32),
            pltpu.VMEM((NZ, 2, 16, BS), F32),
            pltpu.VMEM((NB, 256, BS), F32),
            pltpu.VMEM((NZ, 256, BS), F32),
            pltpu.VMEM((256, 4096), BF16),
            pltpu.VMEM((256, 4096), BF16),
            pltpu.VMEM((NX, 8, 8, BS), F32),
            pltpu.VMEM((NX, 8, 8, BS), F32),
            pltpu.VMEM((NB, 8, 8, BS), F32),
            pltpu.SemaphoreType.DMA((6,)),
        ]
        + sems(8, 8, 8, 8, 16, 16, 16, 16, 16, 4, 8, 8),
        compiler_params=pltpu.CompilerParams(
            collective_id=0, has_side_effects=True, vmem_limit_bytes=56 * 2**20
        ),
        name="exchange",
    )(pair_mu, pair_nu, live_counts, three_centre, orbitals, metric)


def solution(mesh):
    in_specs = (
        P("pair", "ri", None, None),
        P("pair"),
        P("pair"),
        P("pair"),
        P("pair", "batch"),
        P("ri", None),
    )
    return jax.shard_map(
        per_device,
        mesh=mesh,
        in_specs=in_specs,
        out_specs=P("pair", ("ri", "batch"), None),
        check_vma=False,
    )
```

time: 103 us -> 86.7 us (0.84)
  Pallas kernels: 94.7 us -> 84.4 us
  local copies, waits for them, and re-layouts: 5.8 us -> 1.47 us
  other arithmetic: 1.73 us -> 0 us
    pallas_call x1, Pallas kernels: 94.7 us -> 84.4 us  [per_device(): pl.pallas_call(kernel, out_shape=jax.ShapeDtypeStruct((SLOTS, 4, BS), F32...]
    unnamed x9 -> x1, local copies, waits for them, and re-layouts: 4.96 us -> 1.47 us
    reduce_max x2 -> x0, other arithmetic: 1.69 us -> none  [the longest x1 0.92 us: per_device(): prev = jnp.max(jnp.where(same, slot[None, :], -1), axis=1)]
where the time goes in v2:
time: 86.7 us; the launch traced here: 86.6 us
  Pallas kernels  84.4 us (97%)
  local copies, waits for them, and re-layouts  1.47 us (2%)
    pallas_call x1, Pallas kernels, per_device(): pl.pallas_call(kernel, out_shape=jax.ShapeDtypeStruct((SLOTS, 4, BS), F32...  84.4 us

profile of v2, /device:TPU:1, one launch (start us, length us, event | category | flops | bytes accessed | tf_op | source)
XLA Modules:
  0.0 86.6 jit_solution(9573972448964739874)
XLA Ops:
  0.7 84.4 %exchange.1 = f32[32,4,128]{2,1,0:T(4,128)} custom-call(s32[32]{0:T(128)} %mu_any.1, s32[32]{0:T(128)} %nu_any.1, s32[1]{0:T(128)S(6)} %copy.8.live_any, f32[32,2,128,128]{3,2,1,0:T(8,128)} %t_any.1, f32[128,128]{1,0:T(8,128)} %c_any.1, f32[2,16]{1,0:T(2,128)} %m_any.1), custom_call_target="tpu_custom_call" | custom-call | tf_op jit(solution)/shard_map/exchange/pallas_call | solution.py:416
  85.1 1.5 %copy.9 = f32[32,4,128]{2,1,0:T(4,128)} copy(f32[32,4,128]{2,1,0:T(4,128)} %exchange.1) | data formatting | bytes 131072

commit v3 on v2

--- a/solution.py
+++ b/solution.py
@@ -13,7 +13,7 @@
 BS = 128
 NY, NZ, NX = 8, 8, 4
 GROUP = 4
-NEAR_FIRST = (1, 7, 2, 6, 3, 5, 4)
+FAR_FIRST = (4, 3, 5, 2, 6, 1, 7)
 
 
 def split(x):
@@ -74,33 +74,48 @@
         return ypos(d) * 2 + 1 - c
 
     class Gather:
-        def __init__(self, own, buf, half, sems):
-            self.buf, self.half, self.sems = buf, half, sems
-            ss, rs, ds, dr = sems
-            self.cp = {d: send(own, buf.at[p], ss.at[i], rs.at[i], ydev(d)) for i, d in enumerate((2, -2, 1, -1))}
-            self.dp = {0: send(own, buf.at[p], ds.at[0], dr.at[0], partner)}
-
-        def relay(self, d):
-            step = d // 2
+        def __init__(self, piece, whole, buf, half, sems):
+            self.piece, self.whole, self.buf, self.half, self.sems = piece, whole, buf, half, sems
+            self.cp, self.dp = {}, {}
+
+        def post(self, key, src, dst, d):
             ss, rs, _, _ = self.sems
-            self.cp[d].wait_recv()
-            n = 4 if step == 1 else 5
-            at = self.buf.at[block(-d)]
-            self.cp[3 * step] = send(at, at, ss.at[n], rs.at[n], ydev(step))
-            rows = pl.ds(0 if step == 1 else self.half, self.half)
-            part = self.buf.at[block(-d), rows]
-            self.cp[4 * step] = send(part, part, ss.at[n + 2], rs.at[n + 2], ydev(d))
-            self.share(d)
-
-        def share(self, d):
+            n = len(self.cp)
+            self.cp[key] = send(src, dst, ss.at[n], rs.at[n], ydev(d))
+
+        def at(self, i, h):
+            return self.buf.at[i, pl.ds(self.half * h, self.half)]
+
+        def far(self, turn):
+            for s in (1, -1):
+                h = turn if s == 1 else 1 - turn
+                self.post((2 * s, h), self.piece(h), self.at(p, h), 2 * s)
+
+        def near(self):
+            for s in (1, -1):
+                self.post(s, self.whole, self.buf.at[p], s)
+            self.share(0, self.whole)
+
+        def relay(self, turn):
+            for s in (1, -1):
+                h = turn if s == 1 else 1 - turn
+                self.cp[2 * s, h].wait_recv()
+                at = self.at(block(-2 * s), h)
+                if turn == 0:
+                    self.post(4 * s, at, at, 2 * s)
+                self.post((3 * s, h), at, at, s)
+            if turn == 1:
+                self.share(2)
+                self.share(-2)
+
+        def share(self, d, src=None):
             _, _, ds, dr = self.sems
             at = self.buf.at[block(-d)]
-            self.dp[d] = send(at, at, ds.at[d % 8], dr.at[d % 8], partner)
+            self.dp[d] = send(at if src is None else src, at, ds.at[d % 8], dr.at[d % 8], partner)
 
         def take(self, d):
-            self.cp[d].wait_recv()
-            if d == 4:
-                self.cp[-4].wait_recv()
+            for key in {1: (1,), -1: (-1,), 3: ((3, 0), (3, 1)), -3: ((-3, 1), (-3, 0)), 4: (4, -4)}[d]:
+                self.cp[key].wait_recv()
             self.share(d)
 
         def shared(self, d):
@@ -121,7 +136,10 @@
         pl.semaphore_signal(barrier, inc=1, device_id=dev, device_id_type=MESH)
     pl.semaphore_wait(barrier, len(peers))
 
-    orbs = Gather(c_any, c_raw, BS // 2, (a_s, a_r, ad_s, ad_r))
+    half = BS // 2
+    orbs = Gather(lambda h: c_any.at[pl.ds(half * h, half)], c_any, c_raw, half, (a_s, a_r, ad_s, ad_r))
+    orbs.far(0)
+    orbs.far(1)
     ins[4].wait()
     col = lax.broadcasted_iota(jnp.int32, (16, 256), 1)
     spot = (col % 16) == lax.broadcasted_iota(jnp.int32, (16, 256), 0)
@@ -131,7 +149,8 @@
             wide = jnp.where((col >= 16 * i) & spot, m_v[pl.ds(j, 1), pl.ds(i, 1)], wide)
         kr_own[pl.ds(16 * j, 16), :] = wide
     kr_all[q] = kr_own[...]
-    m_cp = {d: send(kr_own, kr_all.at[q], m_s.at[d], m_r.at[d], zdev(d)) for d in NEAR_FIRST}
+    m_cp = {d: send(kr_own, kr_all.at[q], m_s.at[d], m_r.at[d], zdev(d)) for d in FAR_FIRST}
+    orbs.near()
 
     for i in (1, 2, 3):
         ins[i].wait()
@@ -169,8 +188,8 @@
 
     ins[5].wait()
     lax.fori_loop(0, 8, split_t, 0)
-    for d in (2, -2):
-        orbs.relay(d)
+    orbs.relay(0)
+    orbs.relay(1)
     for d in (1, -1):
         orbs.take(d)
     lax.fori_loop(8, SLOTS, split_t, 0)
@@ -204,51 +223,52 @@
 
     d_cp = {}
     for off in (4, 3, 5, 2, 6, 1, 7, 0):
-        d_send[off] = run[last_s[other(off)]].reshape(2, BS, BS)
+        d_send[off] = run[last_s[other(off)]]
         d_cp[off] = send(d_send.at[off], d_recv.at[off], d_s.at[off], d_r.at[off], partner)
 
     def add_core(off):
         d_cp[off].wait_recv()
-        d_recv[off] = d_recv[off] + run[last_s[block(off)]].reshape(2, BS, BS)
-
-    half = BS // 2
+        d_recv[off] = d_recv[off] + run[last_s[block(off)]]
+
     g_cp = {}
 
     def pass_on(off, part, way, kind, hop):
-        rows = pl.ds(half * way, half) if kind == 3 else pl.ds(0, BS)
+        rows = pl.ds(part * BS + half * way, half) if kind == 3 else pl.ds(part * BS, BS)
         n = (part * 2 + way) * 4 + kind
         g_cp[part, way, kind] = send(
-            d_recv.at[off, part, rows], ring.at[part, way, kind, rows], g_s.at[n], g_r.at[n],
+            d_recv.at[off, rows], ring.at[way, kind, rows], g_s.at[n], g_r.at[n],
             ydev(hop if way == 0 else -hop),
         )
 
+    def receive(off, part, way, kind):
+        rows = pl.ds(part * BS + half * way, half) if kind == 3 else pl.ds(part * BS, BS)
+        g_cp[part, way, kind].wait_recv()
+        d_recv[off, rows, :] = d_recv[off, rows, :] + ring[way, kind, rows, :]
+
     add_core(4)
-    for part in (0, 1):
-        for way in (0, 1):
-            pass_on(4, part, way, 3, 2)
+    for way in (0, 1):
+        pass_on(4, 0, way, 3, 2)
     for way, off in ((0, 3), (1, 5)):
         add_core(off)
-        for part in (0, 1):
-            pass_on(off, part, way, 0, 1)
+        pass_on(off, 0, way, 0, 1)
+    for way, off in ((0, 3), (1, 5)):
+        pass_on(4, 1, way, 3, 2)
+        pass_on(off, 1, way, 0, 1)
     add_core(2)
     add_core(6)
     for part in (0, 1):
         for way, off in ((0, 2), (1, 6)):
-            g_cp[part, way, 3].wait_recv()
-            rows = pl.ds(half * way, half)
-            d_recv[off, part, rows, :] = d_recv[off, part, rows, :] + ring[part, way, 3, rows, :]
-            g_cp[part, way, 0].wait_recv()
-            d_recv[off, part] = d_recv[off, part] + ring[part, way, 0]
+            receive(off, part, way, 3)
+            receive(off, part, way, 0)
             pass_on(off, part, way, 1, 1)
     add_core(1)
     add_core(7)
     add_core(0)
     for part in (0, 1):
         for way, off in ((0, 1), (1, 7)):
-            g_cp[part, way, 1].wait_recv()
-            d_recv[off, part] = d_recv[off, part] + ring[part, way, 1]
+            receive(off, part, way, 1)
             pass_on(off, part, way, 2, 1)
-    for d in NEAR_FIRST:
+    for d in FAR_FIRST:
         m_cp[d].wait_recv()
     mix_hi, mix_lo = split(kr_all[...].reshape(256, 256))
     mix[0] = mix_hi
@@ -258,8 +278,9 @@
     for part in (0, 1):
         for way in (0, 1):
             g_cp[part, way, 2].wait_recv()
-        ho[part] = d_recv[0, part] + (ring[part, 0, 2] + ring[part, 1, 2])
-        for d in NEAR_FIRST:
+        rows = pl.ds(part * BS, BS)
+        ho[part] = d_recv[0, rows, :] + (ring[0, 2, rows, :] + ring[1, 2, rows, :])
+        for d in FAR_FIRST:
             rows = pl.ds(pl.multiple_of(zpos(d) * 16, 16), 16)
             n = d * 2 + part
             z_cp[n] = send(ho.at[part, rows], hz.at[q, part], z_s.at[n], z_r.at[n], zdev(d))
@@ -268,41 +289,43 @@
     for n in sorted(z_cp):
         z_cp[n].wait_recv()
     hz_hi, hz_lo = split(hz[...].reshape(256, BS))
+
     fitted = mm(mix[0], hz_hi) + (mm(mix[0], hz_lo) + mm(mix[1], hz_hi))
     lb[p] = fitted
     rb[q] = fitted
 
     f_cp = {}
     fd_cp = {}
+    rows_of = 64
 
     def hand_on(axis, way, part, d, kind, hop):
         sign = 1 if way == 0 else -1
         buf, ss, rs = ((lb, fy_s, fy_r), (rb, fz_s, fz_r))[axis]
         i = block(-sign * d) if axis == 0 else zpos(-sign * d)
-        at = buf.at[i, pl.ds(part * BS, BS)]
+        at = buf.at[i, pl.ds(part * rows_of, rows_of)]
         n = (part * 2 + way) * 4 + kind
         dev = ydev(sign * hop) if axis == 0 else zdev(sign * hop)
         f_cp[axis, way, part, kind] = send(at, at, ss.at[n], rs.at[n], dev)
 
     def to_partner(d, part):
-        at = lb.at[block(-d), pl.ds(part * BS, BS)]
-        n = (d % 8) * 2 + part
+        at = lb.at[block(-d), pl.ds(part * rows_of, rows_of)]
+        n = (d % 8) * 4 + part
         fd_cp[d % 8, part] = send(at, at, fd_s.at[n], fd_r.at[n], partner)
 
     def put_left(i, part):
-        hi, lo = split(lb[i, pl.ds(part * BS, BS), :])
+        hi, lo = split(lb[i, pl.ds(part * rows_of, rows_of), :])
         rows = pl.ds(pl.multiple_of(i * 16, 16), 16)
-        for j in range(8):
-            at = (part * 8 + j) * 256
+        for j in range(4):
+            at = (part * 4 + j) * 256
             l_cat[rows, pl.ds(at, BS)] = hi[16 * j : 16 * j + 16]
             l_cat[rows, pl.ds(at + BS, BS)] = lo[16 * j : 16 * j + 16]
 
     def put_right(i, part):
-        hi, lo = split(rb[i, pl.ds(part * BS, BS), :])
+        hi, lo = split(rb[i, pl.ds(part * rows_of, rows_of), :])
         for s, x in enumerate((hi, lo)):
             rows = pl.ds(pl.multiple_of(i * 16 + BS * s, 16), 16)
-            for j in range(8):
-                at = (part * 8 + j) * 256
+            for j in range(4):
+                at = (part * 4 + j) * 256
                 r_cat[rows, pl.ds(at, BS)] = x[16 * j : 16 * j + 16]
                 r_cat[rows, pl.ds(at + BS, BS)] = x[16 * j : 16 * j + 16]
 
@@ -316,58 +339,64 @@
         fd_cp[d % 8, part].wait_recv()
         put_left(other(-d), part)
 
-    for part in (0, 1):
+    def piece(way, turn):
+        return (turn + 2 * way) % 4
+
+    for turn in range(4):
         for way in (0, 1):
             for axis in (0, 1):
-                hand_on(axis, way, part, 0, 0, 1)
-    for part in (0, 1):
+                hand_on(axis, way, piece(way, turn), 0, 0, 1)
+    for part in range(4):
         to_partner(0, part)
-    for part in (0, 1):
+    for part in range(4):
         put(0, 0, part)
         put(1, 0, part)
-    for part in (0, 1):
+    for turn in range(4):
         for way, sign in ((0, 1), (1, -1)):
+            part = piece(way, turn)
             for axis in (0, 1):
                 f_cp[axis, way, part, 0].wait_recv()
                 hand_on(axis, way, part, 1, 1, 1)
-                if axis == 0:
-                    to_partner(sign, part)
-    for part in (0, 1):
+            to_partner(sign, part)
+    for part in range(4):
         for sign in (1, -1):
             for axis in (0, 1):
                 put(axis, sign, part)
         put_shared(0, part)
-    for part in (0, 1):
+    for turn in range(4):
         for way, sign in ((0, 1), (1, -1)):
+            part = piece(way, turn)
             for axis in (0, 1):
                 f_cp[axis, way, part, 1].wait_recv()
+                if turn < 2:
+                    hand_on(axis, way, part, 2, 3, 2)
                 hand_on(axis, way, part, 2, 2, 1)
-                if way == part:
-                    hand_on(axis, way, part, 2, 3, 2)
-                if axis == 0:
-                    to_partner(2 * sign, part)
-    for part in (0, 1):
+            to_partner(2 * sign, part)
+    for part in range(4):
         for sign in (1, -1):
             put_shared(sign, part)
             for axis in (0, 1):
                 put(axis, 2 * sign, part)
-    for part in (0, 1):
-        for kind in (2, 3):
+    for turn in range(4):
+        for kind in (3, 2):
+            if kind == 3 and turn >= 2:
+                continue
             for way, sign in ((0, 1), (1, -1)):
-                if kind == 3 and way != part:
-                    continue
+                part = piece(way, turn)
                 for axis in (0, 1):
                     f_cp[axis, way, part, kind].wait_recv()
                     if axis == 0:
                         to_partner((kind + 1) * sign, part)
                     put(axis, (kind + 1) * sign, part)
+    for part in range(4):
         for d in (2, -2):
             put_shared(d, part)
 
     k_part = None
     for part in (0, 1):
-        for d in (3, -3, 4):
-            put_shared(d, part)
+        for quarter in (2 * part, 2 * part + 1):
+            for d in (3, -3, 4):
+                put_shared(d, quarter)
         lanes = pl.ds(part * 2048, 2048)
         both = mm(l_cat[:, lanes], r_cat[:, lanes], nt=True)
         both = both[:, :BS] + both[:, BS:]
@@ -383,7 +412,7 @@
                 tile = jnp.where(low, pltpu.roll(first, 4, 0), second)
             pk[j, pair] = tile
     x_cp = {}
-    for d in range(1, NX):
+    for d in (2, 1, 3):
         to = lax.rem(b + d, NX)
         x_cp[d] = send(pk.at[to], xr.at[d], x_s.at[d], x_r.at[d], xdev(d))
     drain(3)
@@ -391,9 +420,12 @@
         x_cp[d].wait_recv()
     kf[p] = (pk[b] + xr[1]) + (xr[2] + xr[3])
 
-    cols = Gather(kf.at[p], kf, 4, (k_s, k_r, kd_s, kd_r))
-    for d in (2, -2):
-        cols.relay(d)
+    cols = Gather(lambda h: kf.at[p, pl.ds(4 * h, 4)], kf.at[p], kf, 4, (k_s, k_r, kd_s, kd_r))
+    cols.far(0)
+    cols.far(1)
+    cols.near()
+    cols.relay(0)
+    cols.relay(1)
     for d in (1, -1, 3, -3, 4):
         cols.take(d)
     for d in (0, 2, -2, 1, -1, 3, -3, 4):
@@ -433,9 +465,9 @@
             pltpu.VMEM((32, 256), F32),
             pltpu.VMEM((NZ, 32, 256), F32),
             pltpu.VMEM((2, 256, 256), BF16),
-            pltpu.VMEM((NY, 2, BS, BS), F32),
-            pltpu.VMEM((NY, 2, BS, BS), F32),
-            pltpu.VMEM((2, 2, 4, BS, BS), F32),
+            pltpu.VMEM((NY, 2 * BS, BS), F32),
+            pltpu.VMEM((NY, 2 * BS, BS), F32),
+            pltpu.VMEM((2, 4, 2 * BS, BS), F32),
             pltpu.VMEM((2, BS, BS), F32),
             pltpu.VMEM((NZ, 2, 16, BS), F32),
             pltpu.VMEM((NB, 256, BS), F32),
@@ -447,7 +479,7 @@
             pltpu.VMEM((NB, 8, 8, BS), F32),
             pltpu.SemaphoreType.DMA((6,)),
         ]
-        + sems(8, 8, 8, 8, 16, 16, 16, 16, 16, 4, 8, 8),
+        + sems(12, 8, 8, 8, 16, 16, 32, 32, 32, 4, 12, 8),
         compiler_params=pltpu.CompilerParams(
             collective_id=0, has_side_effects=True, vmem_limit_bytes=56 * 2**20
         ),

time: 86.7 us -> 85.1 us (0.982)
  Pallas kernels: 84.4 us -> 82.8 us
    pallas_call x1, Pallas kernels: 84.4 us -> 82.8 us  [per_device(): pl.pallas_call(kernel, out_shape=jax.ShapeDtypeStruct((SLOTS, 4, BS), F32...]
where the time goes in v3:
time: 85.1 us; the launch traced here: 84.9 us
  Pallas kernels  82.8 us (97%)
  local copies, waits for them, and re-layouts  1.47 us (2%)
    pallas_call x1, Pallas kernels, per_device(): pl.pallas_call(kernel, out_shape=jax.ShapeDtypeStruct((SLOTS, 4, BS), F32...  82.8 us

profile of v3, /device:TPU:1, one launch (start us, length us, event | category | flops | bytes accessed | tf_op | source)
XLA Modules:
  0.0 84.9 jit_solution(14701478660400668714)
XLA Ops:
  0.7 82.8 %exchange.1 = f32[32,4,128]{2,1,0:T(4,128)} custom-call(s32[32]{0:T(128)} %mu_any.1, s32[32]{0:T(128)} %nu_any.1, s32[1]{0:T(128)S(6)} %copy.8.live_any, f32[32,2,128,128]{3,2,1,0:T(8,128)} %t_any.1, f32[128,128]{1,0:T(8,128)} %c_any.1, f32[2,16]{1,0:T(2,128)} %m_any.1), custom_call_target="tpu_custom_call" | custom-call | tf_op jit(solution)/shard_map/exchange/pallas_call | solution.py:448
  83.4 1.5 %copy.9 = f32[32,4,128]{2,1,0:T(4,128)} copy(f32[32,4,128]{2,1,0:T(4,128)} %exchange.1) | data formatting | bytes 131072

commit v4 on v3

--- a/solution.py
+++ b/solution.py
@@ -12,7 +12,7 @@
 NB = 16
 BS = 128
 NY, NZ, NX = 8, 8, 4
-GROUP = 4
+GROUP = 8
 FAR_FIRST = (4, 3, 5, 2, 6, 1, 7)
 
 
@@ -28,7 +28,7 @@
 
 def kernel(
     mu_any, nu_any, live_any, t_any, c_any, m_any, o_ref,
-    mu_s, nu_s, live_s, prev_s, last_s,
+    mu_s, nu_s, live_s, links_s, links_v,
     t_v, t_cat, run, c_raw, c_cat, m_v, kr_own, kr_all, mix, d_send, d_recv, ring, ho, hz, lb, rb, l_cat, r_cat,
     pk, xr, kf,
     in_sem, a_s, a_r, ad_s, ad_r, m_s, m_r, d_s, d_r, g_s, g_r, z_s, z_r,
@@ -141,13 +141,13 @@
     orbs.far(0)
     orbs.far(1)
     ins[4].wait()
-    col = lax.broadcasted_iota(jnp.int32, (16, 256), 1)
-    spot = (col % 16) == lax.broadcasted_iota(jnp.int32, (16, 256), 0)
+    col = lax.broadcasted_iota(jnp.int32, (8, BS), 1)
+    spot = (col % 8) == lax.broadcasted_iota(jnp.int32, (8, BS), 0)
     for j in range(2):
-        wide = jnp.zeros((16, 256), F32)
+        wide = jnp.zeros((8, BS), F32)
         for i in range(16):
-            wide = jnp.where((col >= 16 * i) & spot, m_v[pl.ds(j, 1), pl.ds(i, 1)], wide)
-        kr_own[pl.ds(16 * j, 16), :] = wide
+            wide = jnp.where((col >= 8 * i) & spot, m_v[pl.ds(j, 1), pl.ds(i, 1)], wide)
+        kr_own[pl.ds(8 * j, 8), :] = wide
     kr_all[q] = kr_own[...]
     m_cp = {d: send(kr_own, kr_all.at[q], m_s.at[d], m_r.at[d], zdev(d)) for d in FAR_FIRST}
     orbs.near()
@@ -156,23 +156,25 @@
         ins[i].wait()
     live = live_s[0]
 
-    def link_slot(k, carry):
-        mine = mu_s[k]
-        best = jnp.int32(SLOTS)
-        for j in range(SLOTS):
-            best = jnp.where((mu_s[j] == mine) & (j < k), jnp.int32(j), best)
-        prev_s[k] = best
-        return carry
-
-    def link_block(a, carry):
-        best = jnp.int32(SLOTS)
-        for j in range(SLOTS):
-            best = jnp.where((mu_s[j] == a) & (j < live), jnp.int32(j), best)
-        last_s[a] = best
-        return carry
-
-    lax.fori_loop(0, SLOTS, link_slot, 0)
-    lax.fori_loop(0, NB, link_block, 0)
+    lane = lax.broadcasted_iota(jnp.int32, (SLOTS, BS), 1)
+    sub = lax.broadcasted_iota(jnp.int32, (SLOTS, BS), 0)
+    down, across = jnp.zeros((SLOTS, BS), jnp.int32), lane - SLOTS
+    for k in range(SLOTS):
+        down = jnp.where(sub == k, mu_s[k], down)
+        across = jnp.where(lane == k, mu_s[k], across)
+    found = jnp.where((down == across) & (sub < jnp.where(lane < SLOTS, lane, live)), sub, -1)
+    best = jnp.maximum(jnp.maximum(found[0:8], found[8:16]), jnp.maximum(found[16:24], found[24:32]))
+    for shift in (4, 2, 1):
+        best = jnp.maximum(best, pltpu.roll(best, shift, 0))
+    links_v[...] = jnp.where(best < 0, SLOTS, best)
+    links = pltpu.make_async_copy(links_v, links_s, in_sem.at[6])
+    links.start()
+
+    def prev_of(k):
+        return links_s[0, k]
+
+    def last_of(a):
+        return links_s[0, SLOTS + a]
 
     def take_c(i):
         hi, lo = split(c_raw[i])
@@ -181,18 +183,20 @@
             c_cat[i, pl.ds(BS * j, BS), pl.ds(BS, BS)] = lo
 
     def split_t(k, carry):
-        hi, lo = split(t_v[k].reshape(2 * BS, BS))
-        t_cat[k, :, pl.ds(0, BS)] = hi
-        t_cat[k, :, pl.ds(BS, BS)] = lo
+        for h in (0, 1):
+            hi, lo = split(t_v[k, :, :, h].reshape(BS, BS))
+            t_cat[k, pl.ds(BS * h, BS), pl.ds(0, BS)] = hi
+            t_cat[k, pl.ds(BS * h, BS), pl.ds(BS, BS)] = lo
         return carry
 
     ins[5].wait()
-    lax.fori_loop(0, 8, split_t, 0)
+    lax.fori_loop(0, 12, split_t, 0)
     orbs.relay(0)
     orbs.relay(1)
     for d in (1, -1):
         orbs.take(d)
-    lax.fori_loop(8, SLOTS, split_t, 0)
+    lax.fori_loop(12, SLOTS, split_t, 0)
+    links.wait()
     ins[0].wait()
     take_c(p)
     for d in (2, -2, 1, -1):
@@ -216,19 +220,19 @@
             products.append(both[:, :BS] + both[:, BS:])
         for j in range(GROUP):
             k = g * GROUP + j
-            run[k] = products[j] + run[prev_s[k]]
+            run[k] = products[j] + run[prev_of(k)]
         return carry
 
     lax.fori_loop(0, SLOTS // GROUP, add_slots, 0)
 
     d_cp = {}
     for off in (4, 3, 5, 2, 6, 1, 7, 0):
-        d_send[off] = run[last_s[other(off)]]
+        d_send[off] = run[last_of(other(off))]
         d_cp[off] = send(d_send.at[off], d_recv.at[off], d_s.at[off], d_r.at[off], partner)
 
     def add_core(off):
         d_cp[off].wait_recv()
-        d_recv[off] = d_recv[off] + run[last_s[block(off)]]
+        d_recv[off] = d_recv[off] + run[last_of(block(off))]
 
     g_cp = {}
 
@@ -270,142 +274,114 @@
             pass_on(off, part, way, 2, 1)
     for d in FAR_FIRST:
         m_cp[d].wait_recv()
-    mix_hi, mix_lo = split(kr_all[...].reshape(256, 256))
+    mix_hi, mix_lo = split(kr_all[...].reshape(BS, BS))
     mix[0] = mix_hi
     mix[1] = mix_lo
 
     z_cp = {}
-    for part in (0, 1):
+    for h in (0, 1):
         for way in (0, 1):
-            g_cp[part, way, 2].wait_recv()
-        rows = pl.ds(part * BS, BS)
-        ho[part] = d_recv[0, rows, :] + (ring[0, 2, rows, :] + ring[1, 2, rows, :])
+            g_cp[h, way, 2].wait_recv()
+        rows = pl.ds(h * BS, BS)
+        total = d_recv[0, rows, :] + (ring[0, 2, rows, :] + ring[1, 2, rows, :])
+        ho[h] = total.reshape(2, NZ, 8, BS)
         for d in FAR_FIRST:
-            rows = pl.ds(pl.multiple_of(zpos(d) * 16, 16), 16)
-            n = d * 2 + part
-            z_cp[n] = send(ho.at[part, rows], hz.at[q, part], z_s.at[n], z_r.at[n], zdev(d))
-        hz[q, part] = ho[part, pl.ds(pl.multiple_of(q * 16, 16), 16), :]
+            n = d * 2 + h
+            z_cp[h, d] = send(ho.at[h, :, zpos(d)], hz.at[h, q], z_s.at[n], z_r.at[n], zdev(d))
+        hz[h, q] = ho[h, :, pl.ds(q, 1)].reshape(2, 8, BS)
     drain(14)
-    for n in sorted(z_cp):
-        z_cp[n].wait_recv()
-    hz_hi, hz_lo = split(hz[...].reshape(256, BS))
-
-    fitted = mm(mix[0], hz_hi) + (mm(mix[0], hz_lo) + mm(mix[1], hz_hi))
-    lb[p] = fitted
-    rb[q] = fitted
 
     f_cp = {}
     fd_cp = {}
-    rows_of = 64
-
-    def hand_on(axis, way, part, d, kind, hop):
+    ways = ((0, 1), (1, -1))
+
+    def fit(h):
+        for d in FAR_FIRST:
+            z_cp[h, d].wait_recv()
+        hi, lo = split(hz[h].reshape(BS, BS))
+        fitted = mm(mix[0], hi) + (mm(mix[0], lo) + mm(mix[1], hi))
+        lb[h, p] = fitted
+        rb[q, h] = fitted
+
+    def hand_on(axis, way, h, u, d, kind, hop):
         sign = 1 if way == 0 else -1
-        buf, ss, rs = ((lb, fy_s, fy_r), (rb, fz_s, fz_r))[axis]
-        i = block(-sign * d) if axis == 0 else zpos(-sign * d)
-        at = buf.at[i, pl.ds(part * rows_of, rows_of)]
-        n = (part * 2 + way) * 4 + kind
+        rows = pl.ds(half * u, half)
+        at = lb.at[h, block(-sign * d), rows] if axis == 0 else rb.at[zpos(-sign * d), h, rows]
+        ss, rs = (fy_s, fy_r) if axis == 0 else (fz_s, fz_r)
+        n = ((h * 2 + u) * 2 + way) * 4 + kind
         dev = ydev(sign * hop) if axis == 0 else zdev(sign * hop)
-        f_cp[axis, way, part, kind] = send(at, at, ss.at[n], rs.at[n], dev)
-
-    def to_partner(d, part):
-        at = lb.at[block(-d), pl.ds(part * rows_of, rows_of)]
-        n = (d % 8) * 4 + part
-        fd_cp[d % 8, part] = send(at, at, fd_s.at[n], fd_r.at[n], partner)
-
-    def put_left(i, part):
-        hi, lo = split(lb[i, pl.ds(part * rows_of, rows_of), :])
-        rows = pl.ds(pl.multiple_of(i * 16, 16), 16)
-        for j in range(4):
-            at = (part * 4 + j) * 256
-            l_cat[rows, pl.ds(at, BS)] = hi[16 * j : 16 * j + 16]
-            l_cat[rows, pl.ds(at + BS, BS)] = lo[16 * j : 16 * j + 16]
-
-    def put_right(i, part):
-        hi, lo = split(rb[i, pl.ds(part * rows_of, rows_of), :])
-        for s, x in enumerate((hi, lo)):
-            rows = pl.ds(pl.multiple_of(i * 16 + BS * s, 16), 16)
-            for j in range(4):
-                at = (part * 4 + j) * 256
-                r_cat[rows, pl.ds(at, BS)] = x[16 * j : 16 * j + 16]
-                r_cat[rows, pl.ds(at + BS, BS)] = x[16 * j : 16 * j + 16]
-
-    def put(axis, d, part):
-        if axis == 0:
-            put_left(block(-d), part)
-        else:
-            put_right(zpos(-d), part)
-
-    def put_shared(d, part):
-        fd_cp[d % 8, part].wait_recv()
-        put_left(other(-d), part)
-
-    def piece(way, turn):
-        return (turn + 2 * way) % 4
-
-    for turn in range(4):
-        for way in (0, 1):
-            for axis in (0, 1):
-                hand_on(axis, way, piece(way, turn), 0, 0, 1)
-    for part in range(4):
-        to_partner(0, part)
-    for part in range(4):
-        put(0, 0, part)
-        put(1, 0, part)
-    for turn in range(4):
-        for way, sign in ((0, 1), (1, -1)):
-            part = piece(way, turn)
-            for axis in (0, 1):
-                f_cp[axis, way, part, 0].wait_recv()
-                hand_on(axis, way, part, 1, 1, 1)
-            to_partner(sign, part)
-    for part in range(4):
-        for sign in (1, -1):
-            for axis in (0, 1):
-                put(axis, sign, part)
-        put_shared(0, part)
-    for turn in range(4):
-        for way, sign in ((0, 1), (1, -1)):
-            part = piece(way, turn)
-            for axis in (0, 1):
-                f_cp[axis, way, part, 1].wait_recv()
-                if turn < 2:
-                    hand_on(axis, way, part, 2, 3, 2)
-                hand_on(axis, way, part, 2, 2, 1)
-            to_partner(2 * sign, part)
-    for part in range(4):
-        for sign in (1, -1):
-            put_shared(sign, part)
-            for axis in (0, 1):
-                put(axis, 2 * sign, part)
-    for turn in range(4):
-        for kind in (3, 2):
-            if kind == 3 and turn >= 2:
-                continue
-            for way, sign in ((0, 1), (1, -1)):
-                part = piece(way, turn)
+        f_cp[axis, way, h, u, kind] = send(at, at, ss.at[n], rs.at[n], dev)
+
+    def to_partner(d, h, u):
+        at = lb.at[h, block(-d), pl.ds(half * u, half)]
+        n = (d % 8) * 4 + h * 2 + u
+        fd_cp[d % 8, h, u] = send(at, at, fd_s.at[n], fd_r.at[n], partner)
+
+    def first_hop(h):
+        for turn in (0, 1):
+            for way, sign in ways:
                 for axis in (0, 1):
-                    f_cp[axis, way, part, kind].wait_recv()
-                    if axis == 0:
-                        to_partner((kind + 1) * sign, part)
-                    put(axis, (kind + 1) * sign, part)
-    for part in range(4):
-        for d in (2, -2):
-            put_shared(d, part)
+                    hand_on(axis, way, h, way ^ turn, 0, 0, 1)
+        for u in (0, 1):
+            to_partner(0, h, u)
+
+    def next_hop(h, kind):
+        for turn in (0, 1):
+            for way, sign in ways:
+                u = way ^ turn
+                for axis in (0, 1):
+                    f_cp[axis, way, h, u, kind - 1].wait_recv()
+                    if kind == 2 and turn == 0:
+                        hand_on(axis, way, h, u, 2, 3, 2)
+                    hand_on(axis, way, h, u, kind, kind, 1)
+                to_partner(kind * sign, h, u)
+
+    def last_hop(h):
+        for kind, turn in ((3, 0), (2, 0), (2, 1)):
+            for way, sign in ways:
+                for axis in (0, 1):
+                    f_cp[axis, way, h, way ^ turn, kind].wait_recv()
+                to_partner((kind + 1) * sign, h, way ^ turn)
+
+    def put_left(h):
+        for d in range(8):
+            for u in (0, 1):
+                fd_cp[d, h, u].wait_recv()
+        rows = pl.ds(BS * h, BS)
+        for j in range(16):
+            hi, lo = split(lb[h, :, pl.ds(8 * j, 8), :].reshape(BS, BS))
+            l_cat[rows, pl.ds(256 * j, BS)] = hi
+            l_cat[rows, pl.ds(256 * j + BS, BS)] = lo
+
+    def put_right():
+        for j in range(16):
+            for s, x in enumerate(split(rb[:, :, pl.ds(8 * j, 8), :].reshape(BS, BS))):
+                r_cat[pl.ds(BS * s, BS), pl.ds(256 * j, BS)] = x
+                r_cat[pl.ds(BS * s, BS), pl.ds(256 * j + BS, BS)] = x
+
+    for h in (0, 1):
+        fit(h)
+        first_hop(h)
+    for kind in (1, 2):
+        for h in (0, 1):
+            next_hop(h, kind)
+    for h in (0, 1):
+        last_hop(h)
+    put_left(0)
+    put_right()
+    put_left(1)
 
     k_part = None
     for part in (0, 1):
-        for quarter in (2 * part, 2 * part + 1):
-            for d in (3, -3, 4):
-                put_shared(d, quarter)
         lanes = pl.ds(part * 2048, 2048)
         both = mm(l_cat[:, lanes], r_cat[:, lanes], nt=True)
         both = both[:, :BS] + both[:, BS:]
         k_part = both if part == 0 else k_part + both
-    tiles = k_part.reshape(16, 2, 8, BS)
+    tiles = k_part.reshape(2, 16, 8, BS)
     low = lax.broadcasted_iota(jnp.int32, (8, BS), 0) < 4
     for j in range(NX):
         for pair in range(8):
-            first, second = tiles[2 * pair, j // 2], tiles[2 * pair + 1, j // 2]
+            first, second = tiles[j // 2, 2 * pair], tiles[j // 2, 2 * pair + 1]
             if j % 2 == 0:
                 tile = jnp.where(low, first, pltpu.roll(second, 4, 0))
             else:
@@ -441,6 +417,7 @@
 
 def per_device(three_centre, pair_mu, pair_nu, live_counts, orbitals, metric):
     hbm = pl.BlockSpec(memory_space=pltpu.HBM)
+    tensor = three_centre.reshape(SLOTS, 2, NZ, 2, 8, BS)
 
     def sems(*counts):
         return [pltpu.SemaphoreType.DMA((n,)) for n in counts for _ in range(2)]
@@ -454,37 +431,37 @@
             pltpu.SMEM((SLOTS,), jnp.int32),
             pltpu.SMEM((SLOTS,), jnp.int32),
             pltpu.SMEM((1,), jnp.int32),
-            pltpu.SMEM((SLOTS,), jnp.int32),
-            pltpu.SMEM((NB,), jnp.int32),
-            pltpu.VMEM((SLOTS, 2, BS, BS), F32),
+            pltpu.SMEM((8, BS), jnp.int32),
+            pltpu.VMEM((8, BS), jnp.int32),
+            pltpu.VMEM((SLOTS, 2, NZ, 2, 8, BS), F32),
             pltpu.VMEM((SLOTS, 2 * BS, 2 * BS), BF16),
             pltpu.VMEM((SLOTS + 1, 2 * BS, BS), F32),
             pltpu.VMEM((NB, BS, BS), F32),
             pltpu.VMEM((NB, 2 * BS, 2 * BS), BF16),
             pltpu.VMEM((2, 16), F32),
-            pltpu.VMEM((32, 256), F32),
-            pltpu.VMEM((NZ, 32, 256), F32),
-            pltpu.VMEM((2, 256, 256), BF16),
+            pltpu.VMEM((16, BS), F32),
+            pltpu.VMEM((NZ, 16, BS), F32),
+            pltpu.VMEM((2, BS, BS), BF16),
             pltpu.VMEM((NY, 2 * BS, BS), F32),
             pltpu.VMEM((NY, 2 * BS, BS), F32),
             pltpu.VMEM((2, 4, 2 * BS, BS), F32),
-            pltpu.VMEM((2, BS, BS), F32),
-            pltpu.VMEM((NZ, 2, 16, BS), F32),
-            pltpu.VMEM((NB, 256, BS), F32),
-            pltpu.VMEM((NZ, 256, BS), F32),
+            pltpu.VMEM((2, 2, NZ, 8, BS), F32),
+            pltpu.VMEM((2, NZ, 2, 8, BS), F32),
+            pltpu.VMEM((2, NB, BS, BS), F32),
+            pltpu.VMEM((NZ, 2, BS, BS), F32),
             pltpu.VMEM((256, 4096), BF16),
             pltpu.VMEM((256, 4096), BF16),
             pltpu.VMEM((NX, 8, 8, BS), F32),
             pltpu.VMEM((NX, 8, 8, BS), F32),
             pltpu.VMEM((NB, 8, 8, BS), F32),
-            pltpu.SemaphoreType.DMA((6,)),
+            pltpu.SemaphoreType.DMA((7,)),
         ]
         + sems(12, 8, 8, 8, 16, 16, 32, 32, 32, 4, 12, 8),
         compiler_params=pltpu.CompilerParams(
             collective_id=0, has_side_effects=True, vmem_limit_bytes=56 * 2**20
         ),
         name="exchange",
-    )(pair_mu, pair_nu, live_counts, three_centre, orbitals, metric)
+    )(pair_mu, pair_nu, live_counts, tensor, orbitals, metric)
 
 
 def solution(mesh):

time: 85.1 us -> 83.7 us (0.984)
  Pallas kernels: 82.8 us -> 81.4 us
    pallas_call x1, Pallas kernels: 82.8 us -> 81.4 us  [per_device(): pl.pallas_call(kernel, out_shape=jax.ShapeDtypeStruct((SLOTS, 4, BS), F32...]
where the time goes in v4:
time: 83.7 us; the launch traced here: 83.6 us
  Pallas kernels  81.4 us (97%)
  local copies, waits for them, and re-layouts  1.47 us (2%)
    pallas_call x1, Pallas kernels, per_device(): pl.pallas_call(kernel, out_shape=jax.ShapeDtypeStruct((SLOTS, 4, BS), F32...  81.4 us

profile of v4, /device:TPU:1, one launch (start us, length us, event | category | flops | bytes accessed | tf_op | source)
XLA Modules:
  0.0 83.6 jit_solution(8692910507582908030)
XLA Ops:
  0.7 81.4 %exchange.1 = f32[32,4,128]{2,1,0:T(4,128)} custom-call(s32[32]{0:T(128)} %mu_any.1, s32[32]{0:T(128)} %nu_any.1, s32[1]{0:T(128)S(6)} %copy.8.live_any, f32[32,2,8,2,8,128]{5,4,3,2,1,0:T(8,128)} %bitcast.1, f32[128,128]{1,0:T(8,128)} %c_any.1, f32[2,16]{1,0:T(2,128)} %m_any.1), custom_call_target="tpu_custom_call" | custom-call | tf_op jit(solution)/shard_map/exchange/pallas_call | solution.py:425
  82.1 1.5 %copy.9 = f32[32,4,128]{2,1,0:T(4,128)} copy(f32[32,4,128]{2,1,0:T(4,128)} %exchange.1) | data formatting | bytes 131072

commit v5 on v4

--- a/solution.py
+++ b/solution.py
@@ -367,33 +367,38 @@
             next_hop(h, kind)
     for h in (0, 1):
         last_hop(h)
+
+    low = lax.broadcasted_iota(jnp.int32, (8, BS), 0) < 4
+
+    def x_copy(j, d, dev):
+        return pltpu.make_async_remote_copy(
+            src_ref=pk.at[j], dst_ref=xr.at[d], send_sem=x_s.at[d], recv_sem=x_r.at[d], device_id=dev, device_id_type=MESH
+        )
+
+    def exchange(h):
+        both = mm(l_cat[pl.ds(BS * h, BS), :], r_cat[...], nt=True)
+        tiles = (both[:, :BS] + both[:, BS:]).reshape(16, 8, BS)
+        for j in (2 * h, 2 * h + 1):
+            for pair in range(8):
+                first, second = tiles[2 * pair], tiles[2 * pair + 1]
+                if j % 2 == 0:
+                    tile = jnp.where(low, first, pltpu.roll(second, 4, 0))
+                else:
+                    tile = jnp.where(low, pltpu.roll(first, 4, 0), second)
+                pk[j, pair] = tile
+
+            @pl.when(b != j)
+            def _():
+                x_copy(j, lax.rem(j - b + NX, NX), (p, q, jnp.int32(j))).start()
+
     put_left(0)
     put_right()
+    exchange(0)
     put_left(1)
-
-    k_part = None
-    for part in (0, 1):
-        lanes = pl.ds(part * 2048, 2048)
-        both = mm(l_cat[:, lanes], r_cat[:, lanes], nt=True)
-        both = both[:, :BS] + both[:, BS:]
-        k_part = both if part == 0 else k_part + both
-    tiles = k_part.reshape(2, 16, 8, BS)
-    low = lax.broadcasted_iota(jnp.int32, (8, BS), 0) < 4
-    for j in range(NX):
-        for pair in range(8):
-            first, second = tiles[j // 2, 2 * pair], tiles[j // 2, 2 * pair + 1]
-            if j % 2 == 0:
-                tile = jnp.where(low, first, pltpu.roll(second, 4, 0))
-            else:
-                tile = jnp.where(low, pltpu.roll(first, 4, 0), second)
-            pk[j, pair] = tile
-    x_cp = {}
-    for d in (2, 1, 3):
-        to = lax.rem(b + d, NX)
-        x_cp[d] = send(pk.at[to], xr.at[d], x_s.at[d], x_r.at[d], xdev(d))
-    drain(3)
+    exchange(1)
+    drain()
     for d in range(1, NX):
-        x_cp[d].wait_recv()
+        x_copy(0, d, xdev(d)).wait_recv()
     kf[p] = (pk[b] + xr[1]) + (xr[2] + xr[3])
 
     cols = Gather(lambda h: kf.at[p, pl.ds(4 * h, 4)], kf.at[p], kf, 4, (k_s, k_r, kd_s, kd_r))
@@ -412,6 +417,8 @@
         tile = kf[nu_s[k], mu >> 1]
         rows = jnp.where(mu & 1 == 1, tile[4:8], tile[0:4])
         o_ref[k] = jnp.where(k < live, rows, jnp.zeros_like(rows))
+    for d in range(1, NX):
+        x_copy(0, d, xdev(d)).wait_send()
     drain()
 
 

time: 83.7 us -> 82.6 us (0.987)
  Pallas kernels: 81.4 us -> 80.3 us
    pallas_call x1, Pallas kernels: 81.4 us -> 80.3 us  [per_device(): pl.pallas_call(kernel, out_shape=jax.ShapeDtypeStruct((SLOTS, 4, BS), F32...]
where the time goes in v5:
time: 82.6 us; the launch traced here: 82.5 us
  Pallas kernels  80.3 us (97%)
  local copies, waits for them, and re-layouts  1.47 us (2%)
    pallas_call x1, Pallas kernels, per_device(): pl.pallas_call(kernel, out_shape=jax.ShapeDtypeStruct((SLOTS, 4, BS), F32...  80.3 us

profile of v5, /device:TPU:1, one launch (start us, length us, event | category | flops | bytes accessed | tf_op | source)
XLA Modules:
  0.0 82.5 jit_solution(4390063803011306645)
XLA Ops:
  0.7 80.3 %exchange.1 = f32[32,4,128]{2,1,0:T(4,128)} custom-call(s32[32]{0:T(128)} %mu_any.1, s32[32]{0:T(128)} %nu_any.1, s32[1]{0:T(128)S(6)} %copy.8.live_any, f32[32,2,8,2,8,128]{5,4,3,2,1,0:T(8,128)} %bitcast.1, f32[128,128]{1,0:T(8,128)} %c_any.1, f32[2,16]{1,0:T(2,128)} %m_any.1), custom_call_target="tpu_custom_call" | custom-call | tf_op jit(solution)/shard_map/exchange/pallas_call | solution.py:432
  81.0 1.5 %copy.9 = f32[32,4,128]{2,1,0:T(4,128)} copy(f32[32,4,128]{2,1,0:T(4,128)} %exchange.1) | data formatting | bytes 131072

commit v6 on v5

--- a/solution.py
+++ b/solution.py
@@ -207,32 +207,41 @@
     for d in (3, -3, 4):
         orbs.take(d)
         take_c(block(-d))
-    run[SLOTS] = jnp.zeros((2 * BS, BS), F32)
+    for h in (0, 1):
+        run[h, SLOTS] = jnp.zeros((BS, BS), F32)
     for d in (3, -3, 4):
         orbs.shared(d)
         take_c(other(-d))
 
-    def add_slots(g, carry):
-        products = []
-        for j in range(GROUP):
-            k = g * GROUP + j
-            both = mm(t_cat[k], c_cat[nu_s[k]])
-            products.append(both[:, :BS] + both[:, BS:])
-        for j in range(GROUP):
-            k = g * GROUP + j
-            run[k] = products[j] + run[prev_of(k)]
-        return carry
-
-    lax.fori_loop(0, SLOTS // GROUP, add_slots, 0)
-
     d_cp = {}
-    for off in (4, 3, 5, 2, 6, 1, 7, 0):
-        d_send[off] = run[last_of(other(off))]
-        d_cp[off] = send(d_send.at[off], d_recv.at[off], d_s.at[off], d_r.at[off], partner)
-
-    def add_core(off):
-        d_cp[off].wait_recv()
-        d_recv[off] = d_recv[off] + run[last_of(block(off))]
+
+    def half_transform(h):
+        rows = pl.ds(BS * h, BS)
+
+        def add_slots(g, carry):
+            products = []
+            for j in range(GROUP):
+                k = g * GROUP + j
+                both = mm(t_cat[k, rows, :], c_cat[nu_s[k]])
+                products.append(both[:, :BS] + both[:, BS:])
+            for j in range(GROUP):
+                k = g * GROUP + j
+                run[h, k] = products[j] + run[h, prev_of(k)]
+            return carry
+
+        lax.fori_loop(0, SLOTS // GROUP, add_slots, 0)
+
+    def swap_cores(h):
+        rows = pl.ds(BS * h, BS)
+        for off in (4, 3, 5, 2, 6, 1, 7, 0):
+            n = off * 2 + h
+            d_send[off, rows, :] = run[h, last_of(other(off))]
+            d_cp[off, h] = send(d_send.at[off, rows], d_recv.at[off, rows], d_s.at[n], d_r.at[n], partner)
+
+    def add_core(off, h):
+        rows = pl.ds(BS * h, BS)
+        d_cp[off, h].wait_recv()
+        d_recv[off, rows, :] = d_recv[off, rows, :] + run[h, last_of(block(off))]
 
     g_cp = {}
 
@@ -249,25 +258,31 @@
         g_cp[part, way, kind].wait_recv()
         d_recv[off, rows, :] = d_recv[off, rows, :] + ring[way, kind, rows, :]
 
-    add_core(4)
-    for way in (0, 1):
-        pass_on(4, 0, way, 3, 2)
-    for way, off in ((0, 3), (1, 5)):
-        add_core(off)
-        pass_on(off, 0, way, 0, 1)
-    for way, off in ((0, 3), (1, 5)):
-        pass_on(4, 1, way, 3, 2)
-        pass_on(off, 1, way, 0, 1)
-    add_core(2)
-    add_core(6)
+    def first_step(h):
+        add_core(4, h)
+        for way in (0, 1):
+            pass_on(4, h, way, 3, 2)
+        for way, off in ((0, 3), (1, 5)):
+            add_core(off, h)
+            pass_on(off, h, way, 0, 1)
+
+    half_transform(0)
+    swap_cores(0)
+    half_transform(1)
+    first_step(0)
+    swap_cores(1)
+    for off in (2, 6, 1, 7, 0):
+        add_core(off, 0)
+    first_step(1)
+    for off in (2, 6):
+        add_core(off, 1)
     for part in (0, 1):
         for way, off in ((0, 2), (1, 6)):
             receive(off, part, way, 3)
             receive(off, part, way, 0)
             pass_on(off, part, way, 1, 1)
-    add_core(1)
-    add_core(7)
-    add_core(0)
+    for off in (1, 7, 0):
+        add_core(off, 1)
     for part in (0, 1):
         for way, off in ((0, 1), (1, 7)):
             receive(off, part, way, 1)
@@ -442,7 +457,7 @@
             pltpu.VMEM((8, BS), jnp.int32),
             pltpu.VMEM((SLOTS, 2, NZ, 2, 8, BS), F32),
             pltpu.VMEM((SLOTS, 2 * BS, 2 * BS), BF16),
-            pltpu.VMEM((SLOTS + 1, 2 * BS, BS), F32),
+            pltpu.VMEM((2, SLOTS + 1, BS, BS), F32),
             pltpu.VMEM((NB, BS, BS), F32),
             pltpu.VMEM((NB, 2 * BS, 2 * BS), BF16),
             pltpu.VMEM((2, 16), F32),
@@ -463,7 +478,7 @@
             pltpu.VMEM((NB, 8, 8, BS), F32),
             pltpu.SemaphoreType.DMA((7,)),
         ]
-        + sems(12, 8, 8, 8, 16, 16, 32, 32, 32, 4, 12, 8),
+        + sems(12, 8, 8, 16, 16, 16, 32, 32, 32, 4, 12, 8),
         compiler_params=pltpu.CompilerParams(
             collective_id=0, has_side_effects=True, vmem_limit_bytes=56 * 2**20
         ),

time: 82.6 us -> 82.3 us (level)
  no operation moved by 1% of the time
where the time goes in v6:
time: 82.3 us; the launch traced here: 82.1 us
  Pallas kernels  80 us (97%)
  local copies, waits for them, and re-layouts  1.47 us (2%)
    pallas_call x1, Pallas kernels, per_device(): pl.pallas_call(kernel, out_shape=jax.ShapeDtypeStruct((SLOTS, 4, BS), F32...  80 us

profile of v6, /device:TPU:1, one launch (start us, length us, event | category | flops | bytes accessed | tf_op | source)
XLA Modules:
  0.0 82.1 jit_solution(7423575808720512654)
XLA Ops:
  0.7 80.0 %exchange.1 = f32[32,4,128]{2,1,0:T(4,128)} custom-call(s32[32]{0:T(128)} %mu_any.1, s32[32]{0:T(128)} %nu_any.1, s32[1]{0:T(128)S(6)} %copy.8.live_any, f32[32,2,8,2,8,128]{5,4,3,2,1,0:T(8,128)} %bitcast.1, f32[128,128]{1,0:T(8,128)} %c_any.1, f32[2,16]{1,0:T(2,128)} %m_any.1), custom_call_target="tpu_custom_call" | custom-call | tf_op jit(solution)/shard_map/exchange/pallas_call | solution.py:447
  80.6 1.5 %copy.9 = f32[32,4,128]{2,1,0:T(4,128)} copy(f32[32,4,128]{2,1,0:T(4,128)} %exchange.1) | data formatting | bytes 131072
